TPU v7x, 32 devices: a whole 2x2x4 slice. The times are simulated.
32 devices in a mesh: seq: 16 (over z, y, x), chan: 2 (over core).
Axes of the slice: x: 2, y: 2, z: 4, core: 2. Of those that a mesh axis runs over, the one named last changes fastest.
Arguments:
- inputs: bfloat16 [3, 64, 4096], P(None, 'chan', 'seq'), may hold values from -6 to 6
- short_weights: float32 [3, 3, 64], P(None, None, 'chan'), may hold values from -3 to 3
- filters: float32 [32, 4096], P(None, 'seq'), may hold values from -1.2 to 1.2
- skip: float32 [64], P('chan'), may hold values from -4 to 4
- grad_out: bfloat16 [64, 4096], P('chan', 'seq'), may hold values from -7.5 to 7.5
Outputs:
- input_grads: float32 [3, 64, 4096], P(None, 'chan', 'seq')
- filter_grad: float32 [32, 4096], P('chan', 'seq')
- skip_grad: float32 [64], P('chan')
- short_grad: float32 [3, 3, 64], P(None, None, 'chan')
All inputs are finite; a program needn't handle non-finite values.
Results may differ from a plain program's by a relative error of at most 0.0003.
Values may be sent and summed in bfloat16 or wider, within the bound.
A program may use at most 64 MiB of HBM per device.

v0:
```python
import math

import jax
import jax.numpy as jnp
from jax import lax
from jax.sharding import PartitionSpec as P

highest = lax.Precision.HIGHEST


def shifted(block, axis, distance):
    devices = range(lax.axis_size(axis))
    route = [(i - distance, i) for i in devices if i - distance in devices]
    return lax.ppermute(block, axis, route)


def angle_table(rows, cols, period, sign):
    grid = (
        jnp.arange(rows, dtype=jnp.int32)[:, None]
        * jnp.arange(cols, dtype=jnp.int32)[None, :]
        % period
    )
    angle = sign * 2.0 * math.pi / period * grid.astype(jnp.float32)
    return (jnp.cos(angle), jnp.sin(angle))


def rotate(real_part, imag_part, cosine, sine):
    return (real_part * cosine - imag_part * sine, real_part * sine + imag_part * cosine)


def transform_last(real_part, imag_part, sign):
    length = real_part.shape[-1]
    if length <= 128 or length % 64 != 0:
        cosine, sine = angle_table(length, length, length, sign)
        new_real = jnp.dot(real_part, cosine, precision=highest) - jnp.dot(
            imag_part, sine, precision=highest
        )
        new_imag = jnp.dot(real_part, sine, precision=highest) + jnp.dot(
            imag_part, cosine, precision=highest
        )
        return (new_real, new_imag)
    outer = 64
    inner = length // outer
    leading = real_part.shape[:-1]
    real_part = jnp.swapaxes(real_part.reshape(leading + (inner, outer)), -1, -2)
    imag_part = jnp.swapaxes(imag_part.reshape(leading + (inner, outer)), -1, -2)
    real_part, imag_part = transform_last(real_part, imag_part, sign)
    cosine, sine = angle_table(outer, inner, length, sign)
    real_part, imag_part = rotate(real_part, imag_part, cosine, sine)
    cosine, sine = angle_table(outer, outer, outer, sign)
    new_real = jnp.einsum("...jk,jl->...lk", real_part, cosine, precision=highest) - jnp.einsum(
        "...jk,jl->...lk", imag_part, sine, precision=highest
    )
    new_imag = jnp.einsum("...jk,jl->...lk", real_part, sine, precision=highest) + jnp.einsum(
        "...jk,jl->...lk", imag_part, cosine, precision=highest
    )
    return (new_real.reshape(leading + (length,)), new_imag.reshape(leading + (length,)))


def forward_spectrum(stacked):
    parts = lax.axis_size("seq")
    rank = lax.axis_index("seq")
    span = stacked.shape[2]
    width = span // parts
    period = 2 * span * parts
    rows = lax.all_to_all(stacked[:, :, None, :], "seq", split_axis=3, concat_axis=2, tiled=True)
    cosine, sine = angle_table(parts, 2 * parts, 2 * parts, -1.0)
    real_part = jnp.einsum("bcpm,pq->bcqm", rows, cosine, precision=highest)
    imag_part = jnp.einsum("bcpm,pq->bcqm", rows, sine, precision=highest)
    column = rank * width + jnp.arange(width, dtype=jnp.int32)
    grid = jnp.arange(2 * parts, dtype=jnp.int32)[:, None] * column[None, :] % period
    angle = -2.0 * math.pi / period * grid.astype(jnp.float32)
    real_part, imag_part = rotate(real_part, imag_part, jnp.cos(angle), jnp.sin(angle))
    real_part, imag_part = (
        lax.all_to_all(real_part, "seq", split_axis=2, concat_axis=3, tiled=True),
        lax.all_to_all(imag_part, "seq", split_axis=2, concat_axis=3, tiled=True),
    )
    return transform_last(real_part, imag_part, -1.0)


def inverse_start(real_part, imag_part):
    parts = lax.axis_size("seq")
    rank = lax.axis_index("seq")
    span = real_part.shape[3]
    period = 2 * span * parts
    real_part, imag_part = transform_last(real_part, imag_part, 1.0)
    residue = 2 * rank + jnp.arange(2, dtype=jnp.int32)
    grid = residue[:, None] * jnp.arange(span, dtype=jnp.int32)[None, :] % period
    angle = 2.0 * math.pi / period * grid.astype(jnp.float32)
    return rotate(real_part, imag_part, jnp.cos(angle), jnp.sin(angle))


def inverse_finish(real_part, imag_part, period):
    parts = lax.axis_size("seq")
    cosine, sine = angle_table(2 * parts, parts, 2 * parts, 1.0)
    new_real = jnp.einsum("bcqm,qp->bcpm", real_part, cosine, precision=highest) - jnp.einsum(
        "bcqm,qp->bcpm", imag_part, sine, precision=highest
    )
    new_imag = jnp.einsum("bcqm,qp->bcpm", real_part, sine, precision=highest) + jnp.einsum(
        "bcqm,qp->bcpm", imag_part, cosine, precision=highest
    )
    return (new_real * (1.0 / period), new_imag * (1.0 / period))


def body(inputs, short_weights, filters, skip, grad_out):
    taps = short_weights.shape[1]
    parts = lax.axis_size("seq")
    groups = lax.axis_size("chan")
    span = inputs.shape[2]
    channels = inputs.shape[1]
    total = span * parts
    period = 2 * total
    border = shifted(inputs[:, :, span - (taps - 1) :], "seq", 1)
    extended = jnp.concatenate([border, inputs], axis=2).astype(jnp.float32)
    mixed = short_weights[:, 0, :, None] * extended[:, :, taps - 1 : taps - 1 + span]
    for offset in range(1, taps):
        start = taps - 1 - offset
        mixed = mixed + short_weights[:, offset, :, None] * extended[:, :, start : start + span]
    query, key_part, value = (mixed[0], mixed[1], mixed[2])
    grad = grad_out.astype(jnp.float32)
    product = key_part * value
    dw = grad * query
    spec_real, spec_imag = forward_spectrum(jnp.stack([product, dw, filters]))
    prod_real, grad_real, filt_real = (spec_real[0], spec_real[1], spec_real[2])
    prod_imag, grad_imag, filt_imag = (spec_imag[0], spec_imag[1], spec_imag[2])
    conv_real = filt_real * prod_real - filt_imag * prod_imag
    conv_imag = filt_real * prod_imag + filt_imag * prod_real
    back_real = grad_real * filt_real + grad_imag * filt_imag
    back_imag = grad_imag * filt_real - grad_real * filt_imag
    corr_real = grad_real * prod_real + grad_imag * prod_imag
    corr_imag = grad_imag * prod_real - grad_real * prod_imag
    start_real, start_imag = inverse_start(
        jnp.stack([conv_real, back_real, corr_real]), jnp.stack([conv_imag, back_imag, corr_imag])
    )
    start_real, start_imag = (
        lax.all_to_all(start_real, "seq", split_axis=3, concat_axis=2, tiled=True),
        lax.all_to_all(start_imag, "seq", split_axis=3, concat_axis=2, tiled=True),
    )
    result, unused = inverse_finish(start_real, start_imag, period)
    fields = lax.all_to_all(result, "seq", split_axis=2, concat_axis=3, tiled=True).reshape(
        3, channels, span
    )
    conv_out = fields[0] + skip[:, None] * product
    dz = fields[1] + skip[:, None] * dw
    filter_grad = lax.psum_scatter(
        fields[2] * (total * groups) ** (-0.5), "chan", scatter_dimension=0, tiled=True
    )
    grads = jnp.stack([grad * conv_out, dz * value, dz * key_part])
    after = shifted(grads[:, :, : taps - 1], "seq", -1)
    grad_ext = jnp.concatenate([grads, after], axis=2)
    in_grads = short_weights[:, 0, :, None] * grads
    for offset in range(1, taps):
        in_grads = (
            in_grads + short_weights[:, offset, :, None] * grad_ext[:, :, offset : offset + span]
        )
    short_rows = []
    for offset in range(taps):
        start = taps - 1 - offset
        short_rows.append(jnp.sum(grads * extended[:, :, start : start + span], axis=2))
    short_part = jnp.stack(short_rows, axis=1)
    skip_part = jnp.sum(dw * product, axis=1)
    short_sum, skip_sum = lax.psum((short_part, skip_part), "seq")
    scale = total ** (-0.5)
    return (in_grads, filter_grad, skip_sum * scale, short_sum * scale)


def solution(mesh):
    placed = (
        P(None, "chan", "seq"),
        P(None, None, "chan"),
        P(None, "seq"),
        P("chan"),
        P("chan", "seq"),
    )
    return jax.shard_map(
        body,
        mesh=mesh,
        in_specs=placed,
        out_specs=(P(None, "chan", "seq"), P("chan", "seq"), P("chan"), P(None, None, "chan")),
        check_vma=False,
    )
```

profile of v0, /device:TPU:0, one launch (start us, length us, event | category | flops | bytes accessed | tf_op | source)
XLA Modules:
  0.0 177.3 jit_solution(11577387516223238131)
XLA Ops:
  8.0 4.8 %collective-permute-start = (bf16[3,32,2]{2,1,0:T(8,128)(2,1)S(1)}, bf16[3,32,2]{2,1,0:T(8,128)(2,1)S(1)}, u32[]{:S(2)}, u32[]{:S(2)}) collective-permute-start(bf16[3,32,2]{2,1,0:T(8,128)(2,1)S(1)} %slice.83), channel_id=1, source_target_pairs={{0,2},{2,4},{4,6},{6,8},{8,10},{10,12},{12,14},{14,16},{16,18},{18... | collective-permute-start | bytes 1160 | tf_op jit(solution)/shard_map/ppermute | solution.py:14
  16.7 2.0 %reduce = f32[256,3,32]{2,1,0:T(4,128)S(1)} reduce(f32[256,3,1,32]{3,2,1,0:T(1,128)S(1)} %bitcast.247, f32[]{:T(128)} %broadcast.417), dimensions={2}, to_apply=%bitcast.195.reduce_sub_computation | reduce | bytes 196612
  19.6 7.6 %all-to-all-start = ((f32[16,1,1536]{2,1,0:T(1,128)}), f32[16,1,1536]{2,1,0:T(1,128)S(1)}, u32[]{:S(2)}, u32[]{:S(2)}) async-start(f32[16,1,1536]{2,1,0:T(1,128)} %reshape.517), calls=%async_computation | async-start | bytes 196608 | tf_op jit(solution)/shard_map/all_to_all | solution.py:66
  27.4 7.5 %all-to-all-done = f32[16,1,1536]{2,1,0:T(1,128)S(1)} async-done(((f32[16,1,1536]{2,1,0:T(1,128)}), f32[16,1,1536]{2,1,0:T(1,128)S(1)}, u32[]{:S(2)}, u32[]{:S(2)}) %all-to-all-start) | async-done | bytes 98336 | tf_op jit(solution)/shard_map/all_to_all | solution.py:66
  37.4 1.1 add_bitcast_fusion
  40.0 3.5 %all-to-all-start.1 = ((f32[16,1,3072]{2,1,0:T(1,128)}), f32[16,1,3072]{2,1,0:T(1,128)S(1)}, u32[]{:S(2)}, u32[]{:S(2)}) async-start(f32[16,1,3072]{2,1,0:T(1,128)} %reshape.519), calls=%async_computation.1 | async-start | bytes 393216 | tf_op jit(solution)/shard_map/all_to_all | solution.py:75
  46.4 5.2 %all-to-all-done.1 = f32[16,1,3072]{2,1,0:T(1,128)S(1)} async-done(((f32[16,1,3072]{2,1,0:T(1,128)}), f32[16,1,3072]{2,1,0:T(1,128)S(1)}, u32[]{:S(2)}, u32[]{:S(2)}) %all-to-all-start.1) | async-done | bytes 196640 | tf_op jit(solution)/shard_map/all_to_all | solution.py:75
  51.6 4.4 %all-to-all-start.2 = ((f32[16,1,3072]{2,1,0:T(1,128)}), f32[16,1,3072]{2,1,0:T(1,128)}, u32[]{:S(2)}, u32[]{:S(2)}) async-start(f32[16,1,3072]{2,1,0:T(1,128)} %reshape.521), calls=%async_computation.2 | async-start | bytes 393216 | tf_op jit(solution)/shard_map/all_to_all | solution.py:76
  55.9 1.1 reduce.2
  59.3 4.5 %all-to-all-done.2 = f32[16,1,3072]{2,1,0:T(1,128)} async-done(((f32[16,1,3072]{2,1,0:T(1,128)}), f32[16,1,3072]{2,1,0:T(1,128)}, u32[]{:S(2)}, u32[]{:S(2)}) %all-to-all-start.2) | async-done | bytes 196640 | tf_op jit(solution)/shard_map/all_to_all | solution.py:76
  63.8 2.0 %reduce.3 = f32[16,3072]{1,0:T(8,128)S(1)} reduce(f32[16,1,3072]{2,1,0:T(1,128)} %all-to-all-done.2, f32[]{:T(128)} %broadcast.417), dimensions={1}, to_apply=%all_to_all.69.reduce_sub_computation | reduce | bytes 393220 | tf_op jit(solution)/shard_map/all_to_all | solution.py:76
  76.8 1.2 multiply_add_fusion.1
  82.7 1.5 reshape.525
  84.1 3.5 %all-to-all-start.4 = ((f32[16,1,3072]{2,1,0:T(1,128)}), f32[16,1,3072]{2,1,0:T(1,128)S(1)}, u32[]{:S(2)}, u32[]{:S(2)}) async-start(f32[16,1,3072]{2,1,0:T(1,128)} %reshape.525), calls=%async_computation.4 | async-start | bytes 393216 | tf_op jit(solution)/shard_map/all_to_all | solution.py:137
  88.3 1.5 reshape.523
  89.8 5.9 %all-to-all-done.4 = f32[16,1,3072]{2,1,0:T(1,128)S(1)} async-done(((f32[16,1,3072]{2,1,0:T(1,128)}), f32[16,1,3072]{2,1,0:T(1,128)S(1)}, u32[]{:S(2)}, u32[]{:S(2)}) %all-to-all-start.4) | async-done | bytes 196640 | tf_op jit(solution)/shard_map/all_to_all | solution.py:137
  95.7 3.5 %all-to-all-start.3 = ((f32[16,1,3072]{2,1,0:T(1,128)}), f32[16,1,3072]{2,1,0:T(1,128)S(1)}, u32[]{:S(2)}, u32[]{:S(2)}) async-start(f32[16,1,3072]{2,1,0:T(1,128)} %reshape.523), calls=%async_computation.3 | async-start | bytes 393216 | tf_op jit(solution)/shard_map/all_to_all | solution.py:136
  99.3 1.1 reduce.5
  101.3 6.0 %all-to-all-done.3 = f32[16,1,3072]{2,1,0:T(1,128)S(1)} async-done(((f32[16,1,3072]{2,1,0:T(1,128)}), f32[16,1,3072]{2,1,0:T(1,128)S(1)}, u32[]{:S(2)}, u32[]{:S(2)}) %all-to-all-start.3) | async-done | bytes 196640 | tf_op jit(solution)/shard_map/all_to_all | solution.py:136
  107.3 1.1 reduce.4
  111.1 10.6 %all_to_all.87 = f32[16,1,1536]{2,1,0:T(1,128)S(1)} all-to-all(f32[16,1,1536]{2,1,0:T(1,128)S(1)} %reshape.527), channel_id=1, replica_groups=mesh['seq'=16,'chan'=2] {'seq'}, dimensions={0} | all-to-all | bytes 196608 | tf_op jit(solution)/shard_map/all_to_all | solution.py:140
  123.7 1.3 collective-permute-start.1
  125.8 3.5 %collective-permute-done.1 = f32[3,32,2]{1,2,0:T(2,128)S(1)} collective-permute-done((f32[3,32,2]{1,2,0:T(2,128)S(1)}, f32[3,32,2]{1,2,0:T(2,128)S(1)}, u32[]{:S(2)}, u32[]{:S(2)}) %collective-permute-start.1) | collective-permute-done | bytes 800 | tf_op jit(solution)/shard_map/ppermute | solution.py:14
  129.6 38.9 %all-reduce = (f32[32]{0:T(128)S(1)}, f32[3,3,32]{2,0,1:T(4,128)S(1)}) all-reduce(f32[32]{0:T(128)S(1)} %get-tuple-element.54, f32[3,3,32]{2,0,1:T(4,128)S(1)} %pad_maximum_fusion.3), channel_id=1, replica_groups=mesh['seq'=16,'chan'=2] {'seq'}, use_global_device_ids=true, to_apply=%region_2.3 | all-reduce | flops 320 | bytes 2560 | tf_op jit(solution)/shard_map/psum | solution.py:162
  (133 shorter events, 38.9 us)
Async XLA Ops:
  8.0 5.5 %copy-start.13 = (f32[3,3,32]{2,1,0:T(4,128)S(1)}, f32[3,3,32]{2,1,0:T(4,128)}, u32[]{:S(2)}) copy-start(f32[3,3,32]{2,1,0:T(4,128)} %param.6) | copy-start | bytes 3460
  8.0 6.4 %collective-permute-start = (bf16[3,32,2]{2,1,0:T(8,128)(2,1)S(1)}, bf16[3,32,2]{2,1,0:T(8,128)(2,1)S(1)}, u32[]{:S(2)}, u32[]{:S(2)}) collective-permute-start(bf16[3,32,2]{2,1,0:T(8,128)(2,1)S(1)} %slice.83), channel_id=1, source_target_pairs={{0,2},{2,4},{4,6},{6,8},{8,10},{10,12},{12,14},{14,16},{16,18},{18... | collective-permute-start | bytes 1160 | tf_op jit(solution)/shard_map/ppermute | solution.py:14
  13.5 0.7 copy-start.8
  13.5 0.8 copy-start.2
  13.5 1.1 copy-start.4
  14.3 0.6 copy-start
  15.0 0.8 copy-start.3
  19.6 15.2 %all-to-all-start = ((f32[16,1,1536]{2,1,0:T(1,128)}), f32[16,1,1536]{2,1,0:T(1,128)S(1)}, u32[]{:S(2)}, u32[]{:S(2)}) async-start(f32[16,1,1536]{2,1,0:T(1,128)} %reshape.517), calls=%async_computation | async-start | bytes 196608 | tf_op jit(solution)/shard_map/all_to_all | solution.py:66
  40.0 11.6 %all-to-all-start.1 = ((f32[16,1,3072]{2,1,0:T(1,128)}), f32[16,1,3072]{2,1,0:T(1,128)S(1)}, u32[]{:S(2)}, u32[]{:S(2)}) async-start(f32[16,1,3072]{2,1,0:T(1,128)} %reshape.519), calls=%async_computation.1 | async-start | bytes 393216 | tf_op jit(solution)/shard_map/all_to_all | solution.py:75
  51.6 12.3 %all-to-all-start.2 = ((f32[16,1,3072]{2,1,0:T(1,128)}), f32[16,1,3072]{2,1,0:T(1,128)}, u32[]{:S(2)}, u32[]{:S(2)}) async-start(f32[16,1,3072]{2,1,0:T(1,128)} %reshape.521), calls=%async_computation.2 | async-start | bytes 393216 | tf_op jit(solution)/shard_map/all_to_all | solution.py:76
  66.5 0.9 copy-start.12
  67.4 0.7 copy-start.11
  75.2 0.9 copy-start.15
  76.1 0.7 copy-start.14
  81.1 0.7 copy-start.10
  81.1 0.7 copy-start.9
  84.1 11.6 %all-to-all-start.4 = ((f32[16,1,3072]{2,1,0:T(1,128)}), f32[16,1,3072]{2,1,0:T(1,128)S(1)}, u32[]{:S(2)}, u32[]{:S(2)}) async-start(f32[16,1,3072]{2,1,0:T(1,128)} %reshape.525), calls=%async_computation.4 | async-start | bytes 393216 | tf_op jit(solution)/shard_map/all_to_all | solution.py:137
  95.7 11.6 %all-to-all-start.3 = ((f32[16,1,3072]{2,1,0:T(1,128)}), f32[16,1,3072]{2,1,0:T(1,128)S(1)}, u32[]{:S(2)}, u32[]{:S(2)}) async-start(f32[16,1,3072]{2,1,0:T(1,128)} %reshape.523), calls=%async_computation.3 | async-start | bytes 393216 | tf_op jit(solution)/shard_map/all_to_all | solution.py:136
  99.2 71.2 %reduce-scatter.4.cloned.1.call-start = ((), (), s32[]{:S(2)}) async-start(), calls=%async_computation.7 | async-start | bytes 49152
  122.8 0.8 copy-start.1
  122.8 0.8 copy-start.16
  123.7 5.5 %collective-permute-start.1 = (f32[3,32,2]{1,2,0:T(2,128)S(1)}, f32[3,32,2]{1,2,0:T(2,128)S(1)}, u32[]{:S(2)}, u32[]{:S(2)}) collective-permute-start(f32[3,32,2]{1,2,0:T(2,128)S(1)} %slice.118), channel_id=1, source_target_pairs={{2,0},{4,2},{6,4},{8,6},{10,8},{12,10},{14,12},{16,14},{18,16},{20... | collective-permute-start | bytes 2312 | tf_op jit(solution)/shard_map/ppermute | solution.py:14
  125.7 3.5 %copy-start.5 = (f32[3,32]{1,0:T(4,128)S(1)}, f32[3,32]{1,0:T(4,128)}, u32[]{:S(2)}) copy-start(f32[3,32]{1,0:T(4,128)} %copy-done.4) | copy-start | bytes 1156
  125.8 3.5 %copy-start.7 = (f32[3,1,32]{2,0,1:T(4,128)S(1)}, f32[3,1,32]{2,0,1:T(4,128)}, u32[]{:S(2)}) copy-start(f32[3,1,32]{2,0,1:T(4,128)} %copy-done.6) | copy-start | bytes 1156
  (1 other events, 0.6 us)
Sparse Core Ops, SparseCore 0:
  125.9 6.4 reduce-scatter.3
where the time goes:
time: 178 us; the launch traced here: 177 us
  blocking collectives  49.6 us (28%)
  waiting for transfers between devices  32.7 us (18%)
  starting transfers between devices  28.7 us (16%)
  local copies, waits for them, and re-layouts  23 us (13%)
  matrix products  15.5 us (9%)
  between operations  14.8 us (8%)
  other arithmetic  13 us (7%)
    psum x1, blocking collectives, body(): short_sum, skip_sum = lax.psum((short_part, skip_part), 'seq')  38.9 us
    unnamed x53, local copies, waits for them, and re-layouts  15.8 us
    all_to_all x1, blocking collectives, body(): lax.all_to_all(result, 'seq', split_axis=2, concat_axis=3, tiled=True)  10.6 us
    all_to_all x1, starting transfers between devices, forward_spectrum(): lax.all_to_all(stacked[:, :, None, :], 'seq', split_axis=3, concat_axis=2...  7.57 us
    all_to_all x1, waiting for transfers between devices, forward_spectrum(): lax.all_to_all(stacked[:, :, None, :], 'seq', split_axis=3, concat_axis=2...  7.53 us
    ppermute x2, starting transfers between devices, shifted(): return lax.ppermute(block, axis, route)  6.14 us
    all_to_all x1, waiting for transfers between devices, body(): lax.all_to_all(start_real, 'seq', split_axis=3, concat_axis=2, tiled=True)  6.04 us
    all_to_all x1, waiting for transfers between devices, body(): lax.all_to_all(start_imag, 'seq', split_axis=3, concat_axis=2, tiled=True)  5.95 us
  transfers between devices with their start and end apart: 8, of which 6 were waited for; matrix products, arithmetic and copies ran while one was open for 8% of the time, Pallas kernels for 0%

commit v1 on v0

--- a/solution.py
+++ b/solution.py
@@ -1,8 +1,12 @@
+import functools
 import math
 
 import jax
 import jax.numpy as jnp
+import numpy as np
 from jax import lax
+from jax.experimental import pallas as pl
+from jax.experimental.pallas import tpu as pltpu
 from jax.sharding import PartitionSpec as P
 
 highest = lax.Precision.HIGHEST
@@ -102,7 +106,7 @@
     return (new_real * (1.0 / period), new_imag * (1.0 / period))
 
 
-def body(inputs, short_weights, filters, skip, grad_out):
+def spectral_body(inputs, short_weights, filters, skip, grad_out):
     taps = short_weights.shape[1]
     parts = lax.axis_size("seq")
     groups = lax.axis_size("chan")
@@ -164,6 +168,353 @@
     return (in_grads, filter_grad, skip_sum * scale, short_sum * scale)
 
 
+MESH = pl.DeviceIdType.MESH
+
+
+def split(x):
+    high = x.astype(jnp.bfloat16)
+    return high, (x - high.astype(jnp.float32)).astype(jnp.bfloat16)
+
+
+def split_table(table):
+    table = np.asarray(table, np.float32)
+    high = table.astype(jnp.bfloat16)
+    return high, (table - high.astype(np.float32)).astype(jnp.bfloat16)
+
+
+def tables(parts, span):
+    period = 2 * parts * span
+    u = np.arange(span)
+    angle = 2.0 * np.pi / span * (u[:, None] * u[None, :] % span)
+    wide = np.concatenate([np.cos(angle), np.sin(angle)], axis=1)
+    wide = np.stack(split_table(wide))
+    k = np.arange(parts) + 0.5
+    angle = 2.0 * np.pi / period * k[:, None] * u[None, :]
+    twiddle = np.stack([np.cos(angle), np.sin(angle)]).astype(np.float32)
+    angle = np.pi / parts * k[:, None] * np.arange(parts)[None, :]
+    high, low = split_table(np.concatenate([np.cos(angle), -np.sin(angle)], axis=0))
+    first = np.concatenate([high, high, low], axis=1)
+    last = np.concatenate([np.cos(angle).T, -np.sin(angle).T], axis=1) * (2.0 / period)
+    high, low = split_table(last)
+    last = np.concatenate([high, high, low], axis=1)
+    return wide, twiddle, first, last
+
+
+def dot(a, b):
+    return jnp.dot(a, b, preferred_element_type=jnp.float32)
+
+
+def kernel(
+    parts, groups, x_ref, g_ref, f_ref, sw_ref, sk_ref, wide_ref, tw_ref, first_ref, last_ref,
+    ig_ref, fg_ref, skg_ref, sg_ref,
+    stage, send, recv, wide, gsend, grecv, fsend, frecv, fstage, sems, wide_sem,
+):
+    taps = sw_ref.shape[1]
+    channels, span = f_ref.shape
+    half = span // 2
+    per = channels // parts
+    rows = per * parts
+    total = parts * span
+    me = lax.axis_index("seq")
+    group = lax.axis_index("chan")
+    share = parts // groups
+    target = me // share
+
+    load_wide = pltpu.make_async_copy(wide_ref, wide, wide_sem)
+    load_wide.start()
+
+    barrier = pltpu.get_barrier_semaphore()
+    for i in range(parts):
+        for j in range(groups):
+            if i or j:
+                pl.semaphore_signal(
+                    barrier,
+                    inc=1,
+                    device_id={"seq": (me + i) % parts, "chan": (group + j) % groups},
+                    device_id_type=MESH,
+                )
+
+    fhigh, flow = split(f_ref[...])
+    pieces = [x_ref[0], x_ref[1], x_ref[2], g_ref[...], fhigh, flow]
+    pieces = [p.astype(jnp.float32) for p in pieces]
+    pieces += [jnp.zeros_like(pieces[0])] * 2
+    for a, piece in enumerate(pieces):
+        stage[pl.ds(2 * a, channels, stride=16), :] = piece[:, :half]
+        stage[pl.ds(2 * a + 1, channels, stride=16), :] = piece[:, half:]
+    send[...] = stage[...].astype(jnp.bfloat16).reshape(send.shape)
+    recv[pl.ds(me, 1)] = send[pl.ds(me, 1)]
+
+    pl.semaphore_wait(barrier, parts * groups - 1)
+    for i in range(1, parts):
+        peer = (me + i) % parts
+        pltpu.make_async_remote_copy(
+            src_ref=send.at[peer], dst_ref=recv.at[me], send_sem=sems.at[0], recv_sem=sems.at[1],
+            device_id={"seq": peer}, device_id_type=MESH,
+        ).start()
+
+    def wait_blocks(ref, count, sem):
+        part = ref.at[pl.ds(0, count)]
+        pltpu.make_async_copy(part, part, sem).wait()
+
+    wait_blocks(recv, parts - 1, sems.at[1])
+    stage[...] = recv[...].astype(jnp.float32).reshape(stage.shape)
+
+    def received(a):
+        blocks = []
+        for ch in range(per):
+            blocks.append(
+                jnp.concatenate(
+                    [stage[pl.ds(16 * ch + 2 * a + h, parts, stride=16 * per), :] for h in (0, 1)],
+                    axis=1,
+                )
+            )
+        return jnp.concatenate(blocks, axis=0)
+
+    row = lax.broadcasted_iota(jnp.int32, (rows, span), 0)
+    lane = lax.broadcasted_iota(jnp.int32, (rows, span), 1)
+
+    def delayed(x, j):
+        if j == 0:
+            return x
+        y = pltpu.roll(x, j, 1)
+        z = jnp.where(row % parts == 0, 0.0, pltpu.roll(y, 1, 0))
+        return jnp.where(lane < j, z, y)
+
+    def advanced(x, j):
+        if j == 0:
+            return x
+        y = pltpu.roll(x, span - j, 1)
+        z = jnp.where(row % parts == parts - 1, 0.0, pltpu.roll(y, rows - 1, 0))
+        return jnp.where(lane >= span - j, z, y)
+
+    def per_channel(values):
+        result = jnp.full((rows, span), values[0], jnp.float32)
+        for ch in range(1, per):
+            result = jnp.where(row >= ch * parts, values[ch], result)
+        return result
+
+    weight = [
+        [per_channel([sw_ref[b, j, per * me + ch] for ch in range(per)]) for j in range(taps)]
+        for b in range(3)
+    ]
+    direct = per_channel([sk_ref[per * me + ch] for ch in range(per)])
+
+    signals = [received(a) for a in range(6)]
+    grad = signals[3]
+    filt = signals[4] + signals[5]
+    moved = [[delayed(signals[b], j) for j in range(taps)] for b in range(3)]
+    mixed = []
+    for b in range(3):
+        value = weight[b][0] * moved[b][0]
+        for j in range(1, taps):
+            value = value + weight[b][j] * moved[b][j]
+        mixed.append(value)
+    query, key_part, value = mixed
+    product = key_part * value
+    dw = grad * query
+
+    cosine, sine = tw_ref[0], tw_ref[1]
+    reals, imags = [], []
+    for signal in (product, dw, filt):
+        for ch in range(per):
+            high, low = split(signal[ch * parts : (ch + 1) * parts])
+            spec = dot(first_ref[...], jnp.concatenate([high, low, high], axis=0))
+            re, im = spec[:parts], spec[parts:]
+            reals.append(re * cosine + im * sine)
+            imags.append(im * cosine - re * sine)
+    load_wide.wait()
+
+    def transform(re, im):
+        both = jnp.concatenate([re, im], axis=0)
+        size = both.shape[0]
+        high, low = split(both)
+        result = dot(jnp.concatenate([high, low], axis=0), wide[0])
+        result = result[:size] + result[size:] + dot(high, wide[1])
+        count = size // 2
+        return (
+            result[:count, :span], result[:count, span:],
+            result[count:, :span], result[count:, span:],
+        )
+
+    rc, rs, ic, is_ = transform(jnp.concatenate(reals, axis=0), jnp.concatenate(imags, axis=0))
+    re, im = rc + is_, ic - rs
+    pr, dr, fr = (re[i * rows : (i + 1) * rows] for i in range(3))
+    pi, di, fi = (im[i * rows : (i + 1) * rows] for i in range(3))
+    out_r = jnp.concatenate([dr * pr + di * pi, fr * pr - fi * pi, dr * fr + di * fi], axis=0)
+    out_i = jnp.concatenate([di * pr - dr * pi, fr * pi + fi * pr, di * fr - dr * fi], axis=0)
+    rc, rs, ic, is_ = transform(out_r, out_i)
+    re, im = rc - is_, ic + rs
+
+    def finish(i):
+        blocks = []
+        for ch in range(per):
+            start = (i * per + ch) * parts
+            cr, ci = re[start : start + parts], im[start : start + parts]
+            both = jnp.concatenate([cr * cosine - ci * sine, ci * cosine + cr * sine], axis=0)
+            high, low = split(both)
+            blocks.append(dot(last_ref[...], jnp.concatenate([high, low, high], axis=0)))
+        return jnp.concatenate(blocks, axis=0)
+
+    corr = finish(0) * (total * groups) ** (-0.5)
+    for ch in range(per):
+        block = corr[ch * parts : (ch + 1) * parts]
+        fstage[pl.ds(2 * ch, parts, stride=2 * per), :] = block[:, :half]
+        fstage[pl.ds(2 * ch + 1, parts, stride=2 * per), :] = block[:, half:]
+    for s in range(parts):
+        fsend[s] = fstage[2 * per * s : 2 * per * (s + 1), :]
+    slot = group * share + me % share
+    for i in range(parts):
+        peer = (me + i) % parts
+        remote = pltpu.make_async_remote_copy(
+            src_ref=fsend.at[peer], dst_ref=frecv.at[slot], send_sem=sems.at[2],
+            recv_sem=sems.at[3], device_id={"seq": peer, "chan": target}, device_id_type=MESH,
+        )
+        if i:
+            remote.start()
+        else:
+
+            @pl.when(target != group)
+            def _():
+                remote.start()
+
+            @pl.when(target == group)
+            def _():
+                pltpu.make_async_copy(fsend.at[me], frecv.at[slot], sems.at[3]).start()
+
+    conv_out = finish(1) + direct * product
+    dz = finish(2) + direct * dw
+    grads = [grad * conv_out, dz * value, dz * key_part]
+    for b in range(3):
+        result = weight[b][0] * grads[b]
+        for j in range(1, taps):
+            result = result + weight[b][j] * advanced(grads[b], j)
+        for ch in range(per):
+            block = result[ch * parts : (ch + 1) * parts]
+            stage[pl.ds(8 * ch + 2 * b, parts, stride=8 * per), :] = block[:, :half]
+            stage[pl.ds(8 * ch + 2 * b + 1, parts, stride=8 * per), :] = block[:, half:]
+
+    scale = total ** (-0.5)
+    sums = [grads[b] * moved[b][j] for b in range(3) for j in range(taps)] + [dw * product]
+    pack = half // channels
+    spot = lax.broadcasted_iota(jnp.int32, (1, half), 1)
+    lines = [jnp.zeros((1, half), jnp.float32) for _ in range(2 * per)]
+    for k, array in enumerate(sums):
+        folded = array[:, :half] + array[:, half:]
+        for ch in range(per):
+            block = jnp.sum(folded[ch * parts : (ch + 1) * parts], axis=0, keepdims=True)
+            amount = jnp.sum(block, axis=1, keepdims=True) * scale
+            at = (k % pack) * channels + per * me + ch
+            lines[k // pack] = jnp.where(spot == at, amount, lines[k // pack])
+    for n, line in enumerate(lines):
+        stage[pl.ds(8 * (n // 2) + 6 + n % 2, parts, stride=8 * per), :] = jnp.broadcast_to(
+            line, (parts, half)
+        )
+    gsend[...] = stage[: 8 * per * parts, :].reshape(gsend.shape)
+    grecv[pl.ds(me, 1)] = gsend[pl.ds(me, 1)]
+    for i in range(1, parts):
+        peer = (me + i) % parts
+        pltpu.make_async_remote_copy(
+            src_ref=gsend.at[peer], dst_ref=grecv.at[me], send_sem=sems.at[4],
+            recv_sem=sems.at[5], device_id={"seq": peer}, device_id_type=MESH,
+        ).start()
+
+    wait_blocks(frecv, parts, sems.at[3])
+    both = frecv[:share]
+    for j in range(1, groups):
+        both = both + frecv[j * share : (j + 1) * share]
+    for i in range(share):
+        fstage[2 * per * i : 2 * per * (i + 1), :] = both[i]
+    for h in (0, 1):
+        fg_ref[:, h * half : (h + 1) * half] = fstage[pl.ds(h, share * per, stride=2), :]
+
+    wait_blocks(grecv, parts - 1, sems.at[5])
+    stage[: 8 * per * parts, :] = grecv[...].reshape(8 * per * parts, half)
+    for b in range(3):
+        for h in (0, 1):
+            ig_ref[b, :, h * half : (h + 1) * half] = stage[
+                pl.ds(2 * b + h, channels, stride=8), :
+            ]
+    lines = []
+    for n in range(2 * per):
+        line = stage[pl.ds(8 * (n // 2) + 6 + n % 2, parts, stride=8 * per), :]
+        lines.append(jnp.sum(line, axis=0, keepdims=True))
+    for k in range(3 * taps + 1):
+        start = (k % pack) * channels
+        piece = lines[k // pack][:, start : start + channels]
+        if k < 3 * taps:
+            sg_ref[k // taps, pl.ds(k % taps, 1), :] = piece
+        else:
+            skg_ref[...] = piece
+
+    wait_blocks(send, parts - 1, sems.at[0])
+    wait_blocks(gsend, parts - 1, sems.at[4])
+    wait_blocks(fsend, parts - 1, sems.at[2])
+
+    @pl.when(target != group)
+    def _():
+        wait_blocks(fsend, 1, sems.at[2])
+
+
+def owner_body(inputs, short_weights, filters, skip, grad_out):
+    parts = lax.axis_size("seq")
+    groups = lax.axis_size("chan")
+    taps = short_weights.shape[1]
+    channels, span = grad_out.shape
+    per = channels // parts
+    half = span // 2
+    wide, twiddle, first, last = (jnp.asarray(t) for t in tables(parts, span))
+    vmem = pl.BlockSpec(memory_space=pltpu.VMEM)
+    smem = pl.BlockSpec(memory_space=pltpu.SMEM)
+    anywhere = pl.BlockSpec(memory_space=pl.ANY)
+    f32 = jnp.float32
+    results = pl.pallas_call(
+        functools.partial(kernel, parts, groups),
+        out_shape=(
+            jax.ShapeDtypeStruct((3, channels, span), f32),
+            jax.ShapeDtypeStruct((channels // groups, span), f32),
+            jax.ShapeDtypeStruct((1, channels), f32),
+            jax.ShapeDtypeStruct((3, taps, channels), f32),
+        ),
+        in_specs=[vmem, vmem, vmem, smem, smem, anywhere, vmem, vmem, vmem],
+        out_specs=(vmem, vmem, vmem, vmem),
+        scratch_shapes=[
+            pltpu.VMEM((16 * channels, half), f32),
+            pltpu.VMEM((parts, 16 * per, half), jnp.bfloat16),
+            pltpu.VMEM((parts, 16 * per, half), jnp.bfloat16),
+            pltpu.VMEM(wide.shape, jnp.bfloat16),
+            pltpu.VMEM((parts, 8 * per, half), f32),
+            pltpu.VMEM((parts, 8 * per, half), f32),
+            pltpu.VMEM((parts, 2 * per, half), f32),
+            pltpu.VMEM((parts, 2 * per, half), f32),
+            pltpu.VMEM((2 * channels, half), f32),
+            pltpu.SemaphoreType.DMA((6,)),
+            pltpu.SemaphoreType.DMA,
+        ],
+        compiler_params=pltpu.CompilerParams(
+            collective_id=0, has_side_effects=True, vmem_limit_bytes=32 * 1024 * 1024
+        ),
+        name="owner_convolutions",
+    )(inputs, grad_out, filters, short_weights, skip, wide, twiddle, first, last)
+    in_grads, filter_grad, skip_grad, short_grad = results
+    return in_grads, filter_grad, skip_grad.reshape(channels), short_grad
+
+
+def body(inputs, short_weights, filters, skip, grad_out):
+    parts = lax.axis_size("seq")
+    groups = lax.axis_size("chan")
+    channels, span = grad_out.shape
+    fits = (
+        channels == 2 * parts
+        and filters.shape[0] == channels
+        and span == 256
+        and parts == 16
+        and parts % groups == 0
+        and short_weights.shape[1] <= 4
+    )
+    chosen = owner_body if fits else spectral_body
+    return chosen(inputs, short_weights, filters, skip, grad_out)
+
+
 def solution(mesh):
     placed = (
         P(None, "chan", "seq"),

time: 178 us -> 30.2 us (0.17)
  blocking collectives: 49.6 us -> 0 us
  waiting for transfers between devices: 32.7 us -> 0 us
  starting transfers between devices: 28.7 us -> 0 us
  Pallas kernels: 0 us -> 19.9 us
  matrix products: 15.5 us -> 0 us
  between operations: 14.8 us -> 0.66 us
  local copies, waits for them, and re-layouts: 23 us -> 9.15 us
  other arithmetic: 13 us -> 0 us
    psum x1 -> x0, blocking collectives: 38.9 us -> none  [body(): short_sum, skip_sum = lax.psum((short_part, skip_part), 'seq')]
    all_to_all x5 -> x0, waiting for transfers between devices: 29.3 us -> none  [the longest x1 7.53 us: forward_spectrum(): lax.all_to_all(stacked[:, :, None, :], 'seq', split_axis=3, concat_axis=2...]
    all_to_all x5 -> x0, starting transfers between devices: 22.5 us -> none  [the longest x1 7.57 us: forward_spectrum(): lax.all_to_all(stacked[:, :, None, :], 'seq', split_axis=3, concat_axis=2...]
    pallas_call x0 -> x1, Pallas kernels: none -> 19.9 us  [owner_body(): pl.pallas_call(functools.partial(kernel, parts, groups), out_shape=(jax.S...]
    dot_general x20 -> x0, matrix products: 15.5 us -> none  [the longest x2 2.21 us: transform_last(): jnp.dot(imag_part, cosine, precision=highest)]
    all_to_all x1 -> x0, blocking collectives: 10.6 us -> none  [body(): lax.all_to_all(result, 'seq', split_axis=2, concat_axis=3, tiled=True)]
    all_to_all x6 -> x0, other arithmetic: 7.16 us -> none  [the longest x1 2.04 us: forward_spectrum(): lax.all_to_all(imag_part, 'seq', split_axis=2, concat_axis=3, tiled=True)]
    unnamed x53 -> x22, local copies, waits for them, and re-layouts: 15.8 us -> 9.15 us
  transfers between devices with their start and end apart: 8 -> 0, of which waited for: 6 -> 0; matrix products, arithmetic and copies ran while one was open for 8% -> 0% of each run, Pallas kernels for 0% -> 0%
where the time goes in v1:
time: 30.2 us; the launch traced here: 29.7 us
  Pallas kernels  19.9 us (66%)
  local copies, waits for them, and re-layouts  9.15 us (30%)
  between operations  0.66 us (2%)
    pallas_call x1, Pallas kernels, owner_body(): pl.pallas_call(functools.partial(kernel, parts, groups), out_shape=(jax.S...  19.9 us
    unnamed x22, local copies, waits for them, and re-layouts  9.15 us

profile of v1, /device:TPU:0, one launch (start us, length us, event | category | flops | bytes accessed | tf_op | source)
XLA Modules:
  0.0 29.7 jit_solution(7749940221541437263)
XLA Ops:
  0.6 0.0 copy-start.7
  0.6 0.7 %copy-done.7 = bf16[16,96]{1,0:T(8,128)(2,1)S(1)} copy-done((bf16[16,96]{1,0:T(8,128)(2,1)S(1)}, bf16[16,96]{1,0:T(8,128)(2,1)}, u32[]{:S(2)}) %copy-start.7) | copy-done | bytes 3096
  1.3 0.0 copy-start
  1.3 1.0 %copy-done = bf16[2,256,512]{2,1,0:T(8,128)(2,1)S(1)} copy-done((bf16[2,256,512]{2,1,0:T(8,128)(2,1)S(1)}, bf16[2,256,512]{2,1,0:T(8,128)(2,1)}, u32[]{:S(2)}) %copy-start) | copy-done | bytes 524312
  2.4 0.0 copy-start.1
  2.4 0.8 %copy-done.1 = bf16[3,32,256]{2,1,0:T(8,128)(2,1)S(1)} copy-done((bf16[3,32,256]{2,1,0:T(8,128)(2,1)S(1)}, bf16[3,32,256]{2,1,0:T(8,128)(2,1)}, u32[]{:S(2)}) %copy-start.1) | copy-done | bytes 49176
  3.2 0.0 copy-start.2
  3.2 0.8 %copy-done.2 = f32[32,256]{1,0:T(8,128)S(1)} copy-done((f32[32,256]{1,0:T(8,128)S(1)}, f32[32,256]{1,0:T(8,128)}, u32[]{:S(2)}) %copy-start.2) | copy-done | bytes 32792
  3.9 0.0 copy-start.3
  3.9 0.8 %copy-done.3 = f32[2,16,256]{2,1,0:T(8,128)S(1)} copy-done((f32[2,16,256]{2,1,0:T(8,128)S(1)}, f32[2,16,256]{2,1,0:T(8,128)}, u32[]{:S(2)}) %copy-start.3) | copy-done | bytes 32792
  4.7 0.0 copy-start.4
  4.7 0.7 %copy-done.4 = bf16[32,256]{1,0:T(8,128)(2,1)S(1)} copy-done((bf16[32,256]{1,0:T(8,128)(2,1)S(1)}, bf16[32,256]{1,0:T(8,128)(2,1)}, u32[]{:S(2)}) %copy-start.4) | copy-done | bytes 16408
  5.4 0.0 copy-start.5
  5.4 0.7 %copy-done.5 = bf16[32,48]{1,0:T(8,128)(2,1)S(1)} copy-done((bf16[32,48]{1,0:T(8,128)(2,1)S(1)}, bf16[32,48]{1,0:T(8,128)(2,1)}, u32[]{:S(2)}) %copy-start.5) | copy-done | bytes 3096
  6.1 0.0 copy-start.6
  6.1 0.7 %copy-done.6 = f32[3,3,32]{2,1,0:T(4,128)S(1)} copy-done((f32[3,3,32]{2,1,0:T(4,128)S(1)}, f32[3,3,32]{2,1,0:T(4,128)}, u32[]{:S(2)}) %copy-start.6) | copy-done | bytes 1176
  6.8 0.0 copy-start.8
  6.8 0.7 %copy-done.8 = f32[32]{0:T(128)S(1)} copy-done((f32[32]{0:T(128)S(1)}, f32[32]{0:T(128)}, u32[]{:S(2)}) %copy-start.8) | copy-done | bytes 152
  7.4 19.9 %owner_convolutions.1 = (f32[3,32,256]{2,1,0:T(8,128)S(1)}, f32[16,256]{1,0:T(8,128)S(1)}, f32[1,32]{1,0:T(1,128)S(1)}, f32[3,3,32]{2,1,0:T(4,128)S(1)}) custom-call(bf16[3,32,256]{2,1,0:T(8,128)(2,1)S(1)} %copy-done.1, bf16[32,256]{1,0:T(8,128)(2,1)S(1)} %copy-done.4, f32[32,256]{1,0:T(8,128)S(1)} %copy-done.2, f32[3,3,32]{2,1,0:T(4,128)S(1)} %copy-done.6, ...), custom_call_target="tpu_custom_call" | custom-call | tf_op jit(solution)/shard_map/owner_convolutions/pallas_call | solution.py:470
  27.3 0.6 %copy.17 = f32[3,32,256]{2,1,0:T(8,128)} copy(f32[3,32,256]{2,1,0:T(8,128)S(1)} %get-tuple-element.16) | data formatting | bytes 196608
  28.0 0.6 %copy.18 = f32[16,256]{1,0:T(8,128)} copy(f32[16,256]{1,0:T(8,128)S(1)} %get-tuple-element.17) | data formatting | bytes 32768
  28.6 0.5 %copy.19 = f32[32]{0:T(128)} copy(f32[32]{0:T(128)S(1)} %bitcast.1) | data formatting | bytes 256
  29.1 0.6 %copy.20 = f32[3,3,32]{2,1,0:T(4,128)} copy(f32[3,3,32]{2,1,0:T(4,128)S(1)} %get-tuple-element.19) | data formatting | bytes 2304
Async XLA Ops:
  0.6 0.7 %copy-start.7 = (bf16[16,96]{1,0:T(8,128)(2,1)S(1)}, bf16[16,96]{1,0:T(8,128)(2,1)}, u32[]{:S(2)}) copy-start(bf16[16,96]{1,0:T(8,128)(2,1)} %constant.11.clone.last_ref) | copy-start | bytes 9220
  1.3 1.0 %copy-start = (bf16[2,256,512]{2,1,0:T(8,128)(2,1)S(1)}, bf16[2,256,512]{2,1,0:T(8,128)(2,1)}, u32[]{:S(2)}) copy-start(bf16[2,256,512]{2,1,0:T(8,128)(2,1)} %constant.8.clone.wide_ref) | copy-start | bytes 1572868
  2.4 0.8 %copy-start.1 = (bf16[3,32,256]{2,1,0:T(8,128)(2,1)S(1)}, bf16[3,32,256]{2,1,0:T(8,128)(2,1)}, u32[]{:S(2)}) copy-start(bf16[3,32,256]{2,1,0:T(8,128)(2,1)} %x_ref.1) | copy-start | bytes 147460
  3.2 0.8 %copy-start.2 = (f32[32,256]{1,0:T(8,128)S(1)}, f32[32,256]{1,0:T(8,128)}, u32[]{:S(2)}) copy-start(f32[32,256]{1,0:T(8,128)} %f_ref.1) | copy-start | bytes 98308
  3.9 0.8 %copy-start.3 = (f32[2,16,256]{2,1,0:T(8,128)S(1)}, f32[2,16,256]{2,1,0:T(8,128)}, u32[]{:S(2)}) copy-start(f32[2,16,256]{2,1,0:T(8,128)} %constant.9.clone.tw_ref) | copy-start | bytes 98308
  4.7 0.7 %copy-start.4 = (bf16[32,256]{1,0:T(8,128)(2,1)S(1)}, bf16[32,256]{1,0:T(8,128)(2,1)}, u32[]{:S(2)}) copy-start(bf16[32,256]{1,0:T(8,128)(2,1)} %g_ref.1) | copy-start | bytes 49156
  5.4 0.7 %copy-start.5 = (bf16[32,48]{1,0:T(8,128)(2,1)S(1)}, bf16[32,48]{1,0:T(8,128)(2,1)}, u32[]{:S(2)}) copy-start(bf16[32,48]{1,0:T(8,128)(2,1)} %constant.10.clone.first_ref) | copy-start | bytes 9220
  6.1 0.7 %copy-start.6 = (f32[3,3,32]{2,1,0:T(4,128)S(1)}, f32[3,3,32]{2,1,0:T(4,128)}, u32[]{:S(2)}) copy-start(f32[3,3,32]{2,1,0:T(4,128)} %sw_ref.1) | copy-start | bytes 3460
  6.8 0.7 %copy-start.8 = (f32[32]{0:T(128)S(1)}, f32[32]{0:T(128)}, u32[]{:S(2)}) copy-start(f32[32]{0:T(128)} %sk_ref.1) | copy-start | bytes 388

commit v2 on v1

--- a/solution.py
+++ b/solution.py
@@ -200,14 +200,25 @@
     return wide, twiddle, first, last
 
 
+def partner(me, i):
+    peer = me
+    bit = 1
+    while bit <= i:
+        if i & bit:
+            peer = peer + bit * (1 - 2 * (me // bit % 2))
+        bit *= 2
+    return peer
+
+
 def dot(a, b):
     return jnp.dot(a, b, preferred_element_type=jnp.float32)
 
 
 def kernel(
-    parts, groups, x_ref, g_ref, f_ref, sw_ref, sk_ref, wide_ref, tw_ref, first_ref, last_ref,
-    ig_ref, fg_ref, skg_ref, sg_ref,
-    stage, send, recv, wide, gsend, grecv, fsend, frecv, fstage, sems, wide_sem,
+    parts, groups, x_hbm, g_hbm, f_hbm, sw_hbm, sk_hbm, wide_hbm, tw_hbm, first_hbm, last_hbm,
+    grecv, frecv,
+    x_ref, g_ref, f_ref, sw_ref, sk_ref, wide, tw_ref, first_ref, last_ref,
+    stage, send, recv, gsend, fsend, fstage, sems, load_sems,
 ):
     taps = sw_ref.shape[1]
     channels, span = f_ref.shape
@@ -220,8 +231,15 @@
     share = parts // groups
     target = me // share
 
-    load_wide = pltpu.make_async_copy(wide_ref, wide, wide_sem)
-    load_wide.start()
+    pairs = [
+        (x_hbm, x_ref), (g_hbm, g_ref), (f_hbm, f_ref), (sw_hbm, sw_ref), (sk_hbm, sk_ref),
+        (tw_hbm, tw_ref), (first_hbm, first_ref), (last_hbm, last_ref), (wide_hbm, wide),
+    ]
+    loads = [
+        pltpu.make_async_copy(src, dst, load_sems.at[n]) for n, (src, dst) in enumerate(pairs)
+    ]
+    for load in loads:
+        load.start()
 
     barrier = pltpu.get_barrier_semaphore()
     for i in range(parts):
@@ -234,6 +252,9 @@
                     device_id_type=MESH,
                 )
 
+    for load in loads[:3]:
+        load.wait()
+
     fhigh, flow = split(f_ref[...])
     pieces = [x_ref[0], x_ref[1], x_ref[2], g_ref[...], fhigh, flow]
     pieces = [p.astype(jnp.float32) for p in pieces]
@@ -245,8 +266,8 @@
     recv[pl.ds(me, 1)] = send[pl.ds(me, 1)]
 
     pl.semaphore_wait(barrier, parts * groups - 1)
-    for i in range(1, parts):
-        peer = (me + i) % parts
+    for i in range(parts - 1, 0, -1):
+        peer = partner(me, i)
         pltpu.make_async_remote_copy(
             src_ref=send.at[peer], dst_ref=recv.at[me], send_sem=sems.at[0], recv_sem=sems.at[1],
             device_id={"seq": peer}, device_id_type=MESH,
@@ -255,9 +276,6 @@
     def wait_blocks(ref, count, sem):
         part = ref.at[pl.ds(0, count)]
         pltpu.make_async_copy(part, part, sem).wait()
-
-    wait_blocks(recv, parts - 1, sems.at[1])
-    stage[...] = recv[...].astype(jnp.float32).reshape(stage.shape)
 
     def received(a):
         blocks = []
@@ -293,11 +311,18 @@
             result = jnp.where(row >= ch * parts, values[ch], result)
         return result
 
+    for load in loads[3:5]:
+        load.wait()
     weight = [
         [per_channel([sw_ref[b, j, per * me + ch] for ch in range(per)]) for j in range(taps)]
         for b in range(3)
     ]
     direct = per_channel([sk_ref[per * me + ch] for ch in range(per)])
+
+    for load in loads[5:]:
+        load.wait()
+    wait_blocks(recv, parts - 1, sems.at[1])
+    stage[...] = recv[...].astype(jnp.float32).reshape(stage.shape)
 
     signals = [received(a) for a in range(6)]
     grad = signals[3]
@@ -322,7 +347,6 @@
             re, im = spec[:parts], spec[parts:]
             reals.append(re * cosine + im * sine)
             imags.append(im * cosine - re * sine)
-    load_wide.wait()
 
     def transform(re, im):
         both = jnp.concatenate([re, im], axis=0)
@@ -363,8 +387,8 @@
     for s in range(parts):
         fsend[s] = fstage[2 * per * s : 2 * per * (s + 1), :]
     slot = group * share + me % share
-    for i in range(parts):
-        peer = (me + i) % parts
+    for i in range(parts - 1, -1, -1):
+        peer = partner(me, i)
         remote = pltpu.make_async_remote_copy(
             src_ref=fsend.at[peer], dst_ref=frecv.at[slot], send_sem=sems.at[2],
             recv_sem=sems.at[3], device_id={"seq": peer, "chan": target}, device_id_type=MESH,
@@ -411,14 +435,47 @@
         )
     gsend[...] = stage[: 8 * per * parts, :].reshape(gsend.shape)
     grecv[pl.ds(me, 1)] = gsend[pl.ds(me, 1)]
-    for i in range(1, parts):
-        peer = (me + i) % parts
+    for i in range(parts - 1, 0, -1):
+        peer = partner(me, i)
         pltpu.make_async_remote_copy(
             src_ref=gsend.at[peer], dst_ref=grecv.at[me], send_sem=sems.at[4],
             recv_sem=sems.at[5], device_id={"seq": peer}, device_id_type=MESH,
         ).start()
 
     wait_blocks(frecv, parts, sems.at[3])
+    wait_blocks(grecv, parts - 1, sems.at[5])
+    wait_blocks(send, parts - 1, sems.at[0])
+    wait_blocks(gsend, parts - 1, sems.at[4])
+    wait_blocks(fsend, parts - 1, sems.at[2])
+
+    @pl.when(target != group)
+    def _():
+        wait_blocks(fsend, 1, sems.at[2])
+
+
+def unpack_kernel(
+    groups, taps, grecv, frecv, ig_hbm, fg_hbm, skg_hbm, sg_hbm,
+    stage, fstage, ig_ref, fg_ref, skg_ref, sg_ref, sems,
+):
+    parts = grecv.shape[0]
+    per = grecv.shape[1] // 8
+    half = grecv.shape[2]
+    channels = per * parts
+    share = parts // groups
+    pack = half // channels
+
+    def save(n, src, dst):
+        copy = pltpu.make_async_copy(src, dst, sems.at[n])
+        copy.start()
+        return copy
+
+    stage[...] = grecv[...].reshape(8 * per * parts, half)
+    for b in range(3):
+        for h in (0, 1):
+            ig_ref[b, :, h * half : (h + 1) * half] = stage[
+                pl.ds(2 * b + h, channels, stride=8), :
+            ]
+    saves = [save(0, ig_ref, ig_hbm)]
     both = frecv[:share]
     for j in range(1, groups):
         both = both + frecv[j * share : (j + 1) * share]
@@ -426,14 +483,7 @@
         fstage[2 * per * i : 2 * per * (i + 1), :] = both[i]
     for h in (0, 1):
         fg_ref[:, h * half : (h + 1) * half] = fstage[pl.ds(h, share * per, stride=2), :]
-
-    wait_blocks(grecv, parts - 1, sems.at[5])
-    stage[: 8 * per * parts, :] = grecv[...].reshape(8 * per * parts, half)
-    for b in range(3):
-        for h in (0, 1):
-            ig_ref[b, :, h * half : (h + 1) * half] = stage[
-                pl.ds(2 * b + h, channels, stride=8), :
-            ]
+    saves.append(save(1, fg_ref, fg_hbm))
     lines = []
     for n in range(2 * per):
         line = stage[pl.ds(8 * (n // 2) + 6 + n % 2, parts, stride=8 * per), :]
@@ -445,14 +495,9 @@
             sg_ref[k // taps, pl.ds(k % taps, 1), :] = piece
         else:
             skg_ref[...] = piece
-
-    wait_blocks(send, parts - 1, sems.at[0])
-    wait_blocks(gsend, parts - 1, sems.at[4])
-    wait_blocks(fsend, parts - 1, sems.at[2])
-
-    @pl.when(target != group)
-    def _():
-        wait_blocks(fsend, 1, sems.at[2])
+    saves += [save(2, skg_ref, skg_hbm), save(3, sg_ref, sg_hbm)]
+    for copy in saves:
+        copy.wait()
 
 
 def owner_body(inputs, short_weights, filters, skip, grad_out):
@@ -464,38 +509,63 @@
     half = span // 2
     wide, twiddle, first, last = (jnp.asarray(t) for t in tables(parts, span))
     vmem = pl.BlockSpec(memory_space=pltpu.VMEM)
-    smem = pl.BlockSpec(memory_space=pltpu.SMEM)
-    anywhere = pl.BlockSpec(memory_space=pl.ANY)
+    hbm = pl.BlockSpec(memory_space=pltpu.HBM)
     f32 = jnp.float32
-    results = pl.pallas_call(
+    operands = (
+        inputs, grad_out, filters, short_weights, skip, wide, twiddle, first, last
+    )
+    limit = 60 * 1024 * 1024
+    blocks = jax.ShapeDtypeStruct((parts, 8 * per, half), f32)
+    filter_blocks = jax.ShapeDtypeStruct((parts, 2 * per, half), f32)
+    blocks, filter_blocks = pl.pallas_call(
         functools.partial(kernel, parts, groups),
-        out_shape=(
-            jax.ShapeDtypeStruct((3, channels, span), f32),
-            jax.ShapeDtypeStruct((channels // groups, span), f32),
-            jax.ShapeDtypeStruct((1, channels), f32),
-            jax.ShapeDtypeStruct((3, taps, channels), f32),
-        ),
-        in_specs=[vmem, vmem, vmem, smem, smem, anywhere, vmem, vmem, vmem],
-        out_specs=(vmem, vmem, vmem, vmem),
+        out_shape=(blocks, filter_blocks),
+        in_specs=[hbm] * 9,
+        out_specs=(vmem, vmem),
         scratch_shapes=[
+            pltpu.VMEM(inputs.shape, inputs.dtype),
+            pltpu.VMEM(grad_out.shape, grad_out.dtype),
+            pltpu.VMEM(filters.shape, filters.dtype),
+            pltpu.SMEM(short_weights.shape, f32),
+            pltpu.SMEM(skip.shape, f32),
+            pltpu.VMEM(wide.shape, wide.dtype),
+            pltpu.VMEM(twiddle.shape, twiddle.dtype),
+            pltpu.VMEM(first.shape, first.dtype),
+            pltpu.VMEM(last.shape, last.dtype),
             pltpu.VMEM((16 * channels, half), f32),
             pltpu.VMEM((parts, 16 * per, half), jnp.bfloat16),
             pltpu.VMEM((parts, 16 * per, half), jnp.bfloat16),
-            pltpu.VMEM(wide.shape, jnp.bfloat16),
             pltpu.VMEM((parts, 8 * per, half), f32),
-            pltpu.VMEM((parts, 8 * per, half), f32),
-            pltpu.VMEM((parts, 2 * per, half), f32),
             pltpu.VMEM((parts, 2 * per, half), f32),
             pltpu.VMEM((2 * channels, half), f32),
             pltpu.SemaphoreType.DMA((6,)),
-            pltpu.SemaphoreType.DMA,
+            pltpu.SemaphoreType.DMA((9,)),
         ],
         compiler_params=pltpu.CompilerParams(
-            collective_id=0, has_side_effects=True, vmem_limit_bytes=32 * 1024 * 1024
+            collective_id=0, has_side_effects=True, vmem_limit_bytes=limit
         ),
         name="owner_convolutions",
-    )(inputs, grad_out, filters, short_weights, skip, wide, twiddle, first, last)
-    in_grads, filter_grad, skip_grad, short_grad = results
+    )(*operands)
+    shapes = (
+        jax.ShapeDtypeStruct((3, channels, span), f32),
+        jax.ShapeDtypeStruct((channels // groups, span), f32),
+        jax.ShapeDtypeStruct((1, channels), f32),
+        jax.ShapeDtypeStruct((3, taps, channels), f32),
+    )
+    in_grads, filter_grad, skip_grad, short_grad = pl.pallas_call(
+        functools.partial(unpack_kernel, groups, taps),
+        out_shape=shapes,
+        in_specs=[vmem, vmem],
+        out_specs=(hbm,) * 4,
+        scratch_shapes=[
+            pltpu.VMEM((8 * channels, half), f32),
+            pltpu.VMEM((2 * channels // groups, half), f32),
+            *[pltpu.VMEM(s.shape, f32) for s in shapes],
+            pltpu.SemaphoreType.DMA((4,)),
+        ],
+        compiler_params=pltpu.CompilerParams(vmem_limit_bytes=limit),
+        name="unpack_results",
+    )(blocks, filter_blocks)
     return in_grads, filter_grad, skip_grad.reshape(channels), short_grad
 
 

time: 30.2 us -> 21.5 us (0.71); the launches traced: 29.7 us -> 21.4 us
  local copies, waits for them, and re-layouts: 9.15 us -> 0 us
  Pallas kernels: 19.9 us -> 20.8 us
    unnamed x22 -> x0, local copies, waits for them, and re-layouts: 9.15 us -> none
    pallas_call x1 -> x2, Pallas kernels: 19.9 us -> 20.8 us  [the longest x1 19.1 us: owner_body(): pl.pallas_call(functools.partial(kernel, parts, groups), out_shape=(block...]
where the time goes in v2:
time: 21.5 us; the launch traced here: 21.4 us
  Pallas kernels  20.8 us (97%)
  between operations  0.64 us (3%)
    pallas_call x1, Pallas kernels, owner_body(): pl.pallas_call(functools.partial(kernel, parts, groups), out_shape=(block...  19.1 us
    pallas_call x1, Pallas kernels, owner_body(): pl.pallas_call(functools.partial(unpack_kernel, groups, taps), out_shape=...  1.65 us

profile of v2, /device:TPU:0, one launch (start us, length us, event | category | flops | bytes accessed | tf_op | source)
XLA Modules:
  0.0 21.4 jit_solution(1128107341128727294)
XLA Ops:
  0.6 19.1 %owner_convolutions.1 = (f32[16,16,128]{2,1,0:T(8,128)}, f32[16,4,128]{2,1,0:T(4,128)}) custom-call(bf16[3,32,256]{2,1,0:T(8,128)(2,1)} %x_hbm.1, bf16[32,256]{1,0:T(8,128)(2,1)} %g_hbm.1, f32[32,256]{1,0:T(8,128)} %f_hbm.1, f32[3,3,32]{2,1,0:T(4,128)} %sw_hbm.1, f32[32]{0:T(128)} %sk_hbm.1, bf16[2,256,512]{2,1,0:T(8,128)(2,1)} %constant.8.clone.wide_hbm, ...), custom_call_target="tpu_custom_call" | custom-call | tf_op jit(solution)/shard_map/owner_convolutions/pallas_call | solution.py:520
  19.7 1.7 %unpack_results.1 = (f32[3,32,256]{2,1,0:T(8,128)}, f32[16,256]{1,0:T(8,128)}, f32[1,32]{1,0:T(1,128)}, f32[3,3,32]{2,1,0:T(4,128)}) custom-call(f32[16,16,128]{2,1,0:T(8,128)} %get-tuple-element.10.grecv, f32[16,4,128]{2,1,0:T(4,128)} %get-tuple-element.11.frecv), custom_call_target="tpu_custom_call" | custom-call | tf_op jit(solution)/shard_map/unpack_results/pallas_call | solution.py:555

commit v3 on v2

--- a/solution.py
+++ b/solution.py
@@ -216,9 +216,9 @@
 
 def kernel(
     parts, groups, x_hbm, g_hbm, f_hbm, sw_hbm, sk_hbm, wide_hbm, tw_hbm, first_hbm, last_hbm,
-    grecv, frecv,
+    grecv, frecv, srecv,
     x_ref, g_ref, f_ref, sw_ref, sk_ref, wide, tw_ref, first_ref, last_ref,
-    stage, send, recv, gsend, fsend, fstage, sems, load_sems,
+    stage, send, recv, filt_send, filt_recv, gsend, fsend, ssend, fstage, sems, load_sems,
 ):
     taps = sw_ref.shape[1]
     channels, span = f_ref.shape
@@ -238,51 +238,69 @@
     loads = [
         pltpu.make_async_copy(src, dst, load_sems.at[n]) for n, (src, dst) in enumerate(pairs)
     ]
-    for load in loads:
+    for load in loads[:3]:
         load.start()
 
+    def greet(seq, chan):
+        pl.semaphore_signal(
+            barrier, inc=1, device_id={"seq": seq, "chan": chan}, device_id_type=MESH
+        )
+
     barrier = pltpu.get_barrier_semaphore()
-    for i in range(parts):
-        for j in range(groups):
-            if i or j:
-                pl.semaphore_signal(
-                    barrier,
-                    inc=1,
-                    device_id={"seq": (me + i) % parts, "chan": (group + j) % groups},
-                    device_id_type=MESH,
-                )
-
+    for i in range(parts - 1, 0, -1):
+        greet(partner(me, i), group)
+    for j in range(1, groups):
+        for i in range(share):
+            greet(group * share + i, (group + j) % groups)
+    for load in loads[3:]:
+        load.start()
     for load in loads[:3]:
         load.wait()
 
-    fhigh, flow = split(f_ref[...])
-    pieces = [x_ref[0], x_ref[1], x_ref[2], g_ref[...], fhigh, flow]
-    pieces = [p.astype(jnp.float32) for p in pieces]
-    pieces += [jnp.zeros_like(pieces[0])] * 2
-    for a, piece in enumerate(pieces):
-        stage[pl.ds(2 * a, channels, stride=16), :] = piece[:, :half]
-        stage[pl.ds(2 * a + 1, channels, stride=16), :] = piece[:, half:]
+    for a, piece in enumerate([x_ref[0], x_ref[1], x_ref[2], g_ref[...]]):
+        piece = piece.astype(jnp.float32)
+        for h in (0, 1):
+            stage[pl.ds(2 * a + h, channels, stride=8), :] = piece[:, h * half : (h + 1) * half]
     send[...] = stage[...].astype(jnp.bfloat16).reshape(send.shape)
+    for h in (0, 1):
+        fstage[pl.ds(h, channels, stride=2), :] = f_ref[:, h * half : (h + 1) * half]
+    for s in range(parts):
+        filt_send[s] = fstage[2 * per * s : 2 * per * (s + 1), :]
     recv[pl.ds(me, 1)] = send[pl.ds(me, 1)]
-
-    pl.semaphore_wait(barrier, parts * groups - 1)
+    filt_recv[pl.ds(me, 1)] = filt_send[pl.ds(me, 1)]
+
+    def push(src, dst, n, peer, chan):
+        return pltpu.make_async_remote_copy(
+            src_ref=src, dst_ref=dst, send_sem=sems.at[n], recv_sem=sems.at[n + 1],
+            device_id={"seq": peer, "chan": chan}, device_id_type=MESH,
+        )
+
+    @pl.when(target == group)
+    def _():
+        pl.semaphore_wait(barrier, parts - 1)
+
+    @pl.when(target != group)
+    def _():
+        pl.semaphore_wait(barrier, 2 * parts - 1)
+
     for i in range(parts - 1, 0, -1):
         peer = partner(me, i)
-        pltpu.make_async_remote_copy(
-            src_ref=send.at[peer], dst_ref=recv.at[me], send_sem=sems.at[0], recv_sem=sems.at[1],
-            device_id={"seq": peer}, device_id_type=MESH,
-        ).start()
+        push(send.at[peer], recv.at[me], 0, peer, group).start()
+        push(filt_send.at[peer], filt_recv.at[me], 2, peer, group).start()
 
     def wait_blocks(ref, count, sem):
         part = ref.at[pl.ds(0, count)]
         pltpu.make_async_copy(part, part, sem).wait()
 
-    def received(a):
+    def received(ref, count, a):
         blocks = []
         for ch in range(per):
             blocks.append(
                 jnp.concatenate(
-                    [stage[pl.ds(16 * ch + 2 * a + h, parts, stride=16 * per), :] for h in (0, 1)],
+                    [
+                        ref[pl.ds(count * ch + 2 * a + h, parts, stride=count * per), :]
+                        for h in (0, 1)
+                    ],
                     axis=1,
                 )
             )
@@ -322,11 +340,13 @@
     for load in loads[5:]:
         load.wait()
     wait_blocks(recv, parts - 1, sems.at[1])
+    wait_blocks(filt_recv, parts - 1, sems.at[3])
     stage[...] = recv[...].astype(jnp.float32).reshape(stage.shape)
-
-    signals = [received(a) for a in range(6)]
+    for s in range(parts):
+        fstage[2 * per * s : 2 * per * (s + 1), :] = filt_recv[s]
+    signals = [received(stage, 8, a) for a in range(4)]
+    filt = received(fstage, 2, 0)
     grad = signals[3]
-    filt = signals[4] + signals[5]
     moved = [[delayed(signals[b], j) for j in range(taps)] for b in range(3)]
     mixed = []
     for b in range(3):
@@ -389,10 +409,7 @@
     slot = group * share + me % share
     for i in range(parts - 1, -1, -1):
         peer = partner(me, i)
-        remote = pltpu.make_async_remote_copy(
-            src_ref=fsend.at[peer], dst_ref=frecv.at[slot], send_sem=sems.at[2],
-            recv_sem=sems.at[3], device_id={"seq": peer, "chan": target}, device_id_type=MESH,
-        )
+        remote = push(fsend.at[peer], frecv.at[slot], 4, peer, target)
         if i:
             remote.start()
         else:
@@ -403,7 +420,7 @@
 
             @pl.when(target == group)
             def _():
-                pltpu.make_async_copy(fsend.at[me], frecv.at[slot], sems.at[3]).start()
+                pltpu.make_async_copy(fsend.at[me], frecv.at[slot], sems.at[5]).start()
 
     conv_out = finish(1) + direct * product
     dz = finish(2) + direct * dw
@@ -414,83 +431,82 @@
             result = result + weight[b][j] * advanced(grads[b], j)
         for ch in range(per):
             block = result[ch * parts : (ch + 1) * parts]
-            stage[pl.ds(8 * ch + 2 * b, parts, stride=8 * per), :] = block[:, :half]
-            stage[pl.ds(8 * ch + 2 * b + 1, parts, stride=8 * per), :] = block[:, half:]
+            for h in (0, 1):
+                start = b * parts * 2 * per + 2 * ch + h
+                stage[pl.ds(start, parts, stride=2 * per), :] = block[:, h * half : (h + 1) * half]
+        for s in range(parts):
+            start = (b * parts + s) * 2 * per
+            gsend[b, s] = stage[start : start + 2 * per, :]
+    pltpu.make_async_copy(gsend.at[:, me], grecv.at[:, me], sems.at[7]).start()
+    for i in range(parts - 1, 0, -1):
+        peer = partner(me, i)
+        push(gsend.at[:, peer], grecv.at[:, me], 6, peer, group).start()
 
     scale = total ** (-0.5)
     sums = [grads[b] * moved[b][j] for b in range(3) for j in range(taps)] + [dw * product]
-    pack = half // channels
     spot = lax.broadcasted_iota(jnp.int32, (1, half), 1)
-    lines = [jnp.zeros((1, half), jnp.float32) for _ in range(2 * per)]
+    line = jnp.zeros((1, half), jnp.float32)
     for k, array in enumerate(sums):
         folded = array[:, :half] + array[:, half:]
         for ch in range(per):
             block = jnp.sum(folded[ch * parts : (ch + 1) * parts], axis=0, keepdims=True)
             amount = jnp.sum(block, axis=1, keepdims=True) * scale
-            at = (k % pack) * channels + per * me + ch
-            lines[k // pack] = jnp.where(spot == at, amount, lines[k // pack])
-    for n, line in enumerate(lines):
-        stage[pl.ds(8 * (n // 2) + 6 + n % 2, parts, stride=8 * per), :] = jnp.broadcast_to(
-            line, (parts, half)
-        )
-    gsend[...] = stage[: 8 * per * parts, :].reshape(gsend.shape)
-    grecv[pl.ds(me, 1)] = gsend[pl.ds(me, 1)]
+            line = jnp.where(spot == k * per + per * me + ch, amount, line)
+    ssend[...] = line
+    pltpu.make_async_copy(ssend, srecv.at[me], sems.at[9]).start()
     for i in range(parts - 1, 0, -1):
-        peer = partner(me, i)
-        pltpu.make_async_remote_copy(
-            src_ref=gsend.at[peer], dst_ref=grecv.at[me], send_sem=sems.at[4],
-            recv_sem=sems.at[5], device_id={"seq": peer}, device_id_type=MESH,
-        ).start()
-
-    wait_blocks(frecv, parts, sems.at[3])
-    wait_blocks(grecv, parts - 1, sems.at[5])
+        push(ssend, srecv.at[me], 8, partner(me, i), group).start()
+
+    wait_blocks(frecv, parts, sems.at[5])
+    pltpu.make_async_copy(grecv, grecv, sems.at[7]).wait()
+    wait_blocks(srecv, parts, sems.at[9])
     wait_blocks(send, parts - 1, sems.at[0])
-    wait_blocks(gsend, parts - 1, sems.at[4])
-    wait_blocks(fsend, parts - 1, sems.at[2])
+    wait_blocks(filt_send, parts - 1, sems.at[2])
+    wait_blocks(fsend, parts - 1, sems.at[4])
 
     @pl.when(target != group)
     def _():
-        wait_blocks(fsend, 1, sems.at[2])
+        wait_blocks(fsend, 1, sems.at[4])
+
+    part = gsend.at[:, pl.ds(0, parts - 1)]
+    pltpu.make_async_copy(part, part, sems.at[6]).wait()
+    wait_blocks(srecv, parts - 1, sems.at[8])
 
 
 def unpack_kernel(
-    groups, taps, grecv, frecv, ig_hbm, fg_hbm, skg_hbm, sg_hbm,
-    stage, fstage, ig_ref, fg_ref, skg_ref, sg_ref, sems,
+    groups, parts, grecv, frecv, srecv, ig_hbm, fg_hbm, skg_hbm, sg_hbm,
+    ig_ref, fg_ref, skg_ref, sg_ref, sems,
 ):
-    parts = grecv.shape[0]
-    per = grecv.shape[1] // 8
-    half = grecv.shape[2]
-    channels = per * parts
-    share = parts // groups
-    pack = half // channels
+    taps, channels = sg_ref.shape[1:]
+    half = grecv.shape[1]
+    per = channels // parts
+    share = channels // groups
 
     def save(n, src, dst):
         copy = pltpu.make_async_copy(src, dst, sems.at[n])
         copy.start()
         return copy
 
-    stage[...] = grecv[...].reshape(8 * per * parts, half)
     for b in range(3):
         for h in (0, 1):
-            ig_ref[b, :, h * half : (h + 1) * half] = stage[
-                pl.ds(2 * b + h, channels, stride=8), :
+            ig_ref[b, :, h * half : (h + 1) * half] = grecv[
+                pl.ds(b * 2 * channels + h, channels, stride=2), :
             ]
     saves = [save(0, ig_ref, ig_hbm)]
-    both = frecv[:share]
-    for j in range(1, groups):
-        both = both + frecv[j * share : (j + 1) * share]
-    for i in range(share):
-        fstage[2 * per * i : 2 * per * (i + 1), :] = both[i]
     for h in (0, 1):
-        fg_ref[:, h * half : (h + 1) * half] = fstage[pl.ds(h, share * per, stride=2), :]
+        both = frecv[pl.ds(h, share, stride=2), :]
+        for j in range(1, groups):
+            both = both + frecv[pl.ds(2 * share * j + h, share, stride=2), :]
+        fg_ref[:, h * half : (h + 1) * half] = both
     saves.append(save(1, fg_ref, fg_hbm))
-    lines = []
-    for n in range(2 * per):
-        line = stage[pl.ds(8 * (n // 2) + 6 + n % 2, parts, stride=8 * per), :]
-        lines.append(jnp.sum(line, axis=0, keepdims=True))
+    sums = srecv[...]
+    row = lax.broadcasted_iota(jnp.int32, sums.shape, 0)
+    lane = lax.broadcasted_iota(jnp.int32, sums.shape, 1)
     for k in range(3 * taps + 1):
-        start = (k % pack) * channels
-        piece = lines[k // pack][:, start : start + channels]
+        first = (row + k) * per
+        mine = (lane >= first) & (lane < first + per)
+        line = jnp.sum(jnp.where(mine, sums, 0.0), axis=0, keepdims=True)
+        piece = line[:, k * per : k * per + channels]
         if k < 3 * taps:
             sg_ref[k // taps, pl.ds(k % taps, 1), :] = piece
         else:
@@ -515,13 +531,16 @@
         inputs, grad_out, filters, short_weights, skip, wide, twiddle, first, last
     )
     limit = 60 * 1024 * 1024
-    blocks = jax.ShapeDtypeStruct((parts, 8 * per, half), f32)
-    filter_blocks = jax.ShapeDtypeStruct((parts, 2 * per, half), f32)
-    blocks, filter_blocks = pl.pallas_call(
+    landing = (
+        jax.ShapeDtypeStruct((3, parts, 2 * per, half), f32),
+        jax.ShapeDtypeStruct((parts, 2 * per, half), f32),
+        jax.ShapeDtypeStruct((parts, 1, half), f32),
+    )
+    blocks, filter_blocks, sums = pl.pallas_call(
         functools.partial(kernel, parts, groups),
-        out_shape=(blocks, filter_blocks),
+        out_shape=landing,
         in_specs=[hbm] * 9,
-        out_specs=(vmem, vmem),
+        out_specs=(hbm,) * 3,
         scratch_shapes=[
             pltpu.VMEM(inputs.shape, inputs.dtype),
             pltpu.VMEM(grad_out.shape, grad_out.dtype),
@@ -532,13 +551,16 @@
             pltpu.VMEM(twiddle.shape, twiddle.dtype),
             pltpu.VMEM(first.shape, first.dtype),
             pltpu.VMEM(last.shape, last.dtype),
-            pltpu.VMEM((16 * channels, half), f32),
-            pltpu.VMEM((parts, 16 * per, half), jnp.bfloat16),
-            pltpu.VMEM((parts, 16 * per, half), jnp.bfloat16),
-            pltpu.VMEM((parts, 8 * per, half), f32),
+            pltpu.VMEM((8 * channels, half), f32),
+            pltpu.VMEM((parts, 8 * per, half), jnp.bfloat16),
+            pltpu.VMEM((parts, 8 * per, half), jnp.bfloat16),
             pltpu.VMEM((parts, 2 * per, half), f32),
+            pltpu.VMEM((parts, 2 * per, half), f32),
+            pltpu.VMEM((3, parts, 2 * per, half), f32),
+            pltpu.VMEM((parts, 2 * per, half), f32),
+            pltpu.VMEM((1, half), f32),
             pltpu.VMEM((2 * channels, half), f32),
-            pltpu.SemaphoreType.DMA((6,)),
+            pltpu.SemaphoreType.DMA((10,)),
             pltpu.SemaphoreType.DMA((9,)),
         ],
         compiler_params=pltpu.CompilerParams(
@@ -553,19 +575,21 @@
         jax.ShapeDtypeStruct((3, taps, channels), f32),
     )
     in_grads, filter_grad, skip_grad, short_grad = pl.pallas_call(
-        functools.partial(unpack_kernel, groups, taps),
+        functools.partial(unpack_kernel, groups, parts),
         out_shape=shapes,
-        in_specs=[vmem, vmem],
+        in_specs=[vmem] * 3,
         out_specs=(hbm,) * 4,
         scratch_shapes=[
-            pltpu.VMEM((8 * channels, half), f32),
-            pltpu.VMEM((2 * channels // groups, half), f32),
             *[pltpu.VMEM(s.shape, f32) for s in shapes],
             pltpu.SemaphoreType.DMA((4,)),
         ],
         compiler_params=pltpu.CompilerParams(vmem_limit_bytes=limit),
         name="unpack_results",
-    )(blocks, filter_blocks)
+    )(
+        blocks.reshape(6 * channels, half),
+        filter_blocks.reshape(2 * channels, half),
+        sums.reshape(parts, half),
+    )
     return in_grads, filter_grad, skip_grad.reshape(channels), short_grad
 
 

time: 21.5 us -> 20.9 us (0.972)
  Pallas kernels: 20.8 us -> 20.1 us
    pallas_call x2, Pallas kernels: 20.8 us -> 20.1 us  [the longest x1 18.4 us: owner_body(): pl.pallas_call(functools.partial(kernel, parts, groups), out_shape=landin...]
where the time goes in v3:
time: 20.9 us; the launch traced here: 20.7 us
  Pallas kernels  20.1 us (96%)
  between operations  0.64 us (3%)
    pallas_call x1, Pallas kernels, owner_body(): pl.pallas_call(functools.partial(kernel, parts, groups), out_shape=landin...  18.4 us
    pallas_call x1, Pallas kernels, owner_body(): pl.pallas_call(functools.partial(unpack_kernel, groups, parts), out_shape...  1.65 us

profile of v3, /device:TPU:0, one launch (start us, length us, event | category | flops | bytes accessed | tf_op | source)
XLA Modules:
  0.0 20.7 jit_solution(16638032566980042988)
XLA Ops:
  0.6 18.4 %owner_convolutions.1 = (f32[3,16,4,128]{3,2,1,0:T(4,128)}, f32[16,4,128]{2,1,0:T(4,128)}, f32[16,1,128]{2,1,0:T(1,128)}) custom-call(bf16[3,32,256]{2,1,0:T(8,128)(2,1)} %x_hbm.1, bf16[32,256]{1,0:T(8,128)(2,1)} %g_hbm.1, f32[32,256]{1,0:T(8,128)} %f_hbm.1, f32[3,3,32]{2,1,0:T(4,128)} %sw_hbm.1, f32[32]{0:T(128)} %sk_hbm.1, ...), custom_call_target="tpu_custom_call" | custom-call | tf_op jit(solution)/shard_map/owner_convolutions/pallas_call | solution.py:539
  19.1 1.6 %unpack_results.1 = (f32[3,32,256]{2,1,0:T(8,128)}, f32[16,256]{1,0:T(8,128)}, f32[1,32]{1,0:T(1,128)}, f32[3,3,32]{2,1,0:T(4,128)}) custom-call(f32[192,128]{1,0:T(8,128)} %bitcast.4, f32[64,128]{1,0:T(8,128)} %bitcast.5, f32[16,128]{1,0:T(8,128)} %bitcast.6), custom_call_target="tpu_custom_call" | custom-call | tf_op jit(solution)/shard_map/unpack_results/pallas_call | solution.py:577

commit v4 on v3

--- a/solution.py
+++ b/solution.py
@@ -285,8 +285,10 @@
 
     for i in range(parts - 1, 0, -1):
         peer = partner(me, i)
+        push(filt_send.at[peer], filt_recv.at[me], 2, peer, group).start()
+    for i in range(parts - 1, 0, -1):
+        peer = partner(me, i)
         push(send.at[peer], recv.at[me], 0, peer, group).start()
-        push(filt_send.at[peer], filt_recv.at[me], 2, peer, group).start()
 
     def wait_blocks(ref, count, sem):
         part = ref.at[pl.ds(0, count)]
@@ -339,13 +341,44 @@
 
     for load in loads[5:]:
         load.wait()
-    wait_blocks(recv, parts - 1, sems.at[1])
+    cosine, sine = tw_ref[0], tw_ref[1]
+
+    def transform(re, im):
+        both = jnp.concatenate([re, im], axis=0)
+        size = both.shape[0]
+        high, low = split(both)
+        result = dot(jnp.concatenate([high, low], axis=0), wide[0])
+        result = result[:size] + result[size:] + dot(high, wide[1])
+        count = size // 2
+        return (
+            result[:count, :span], result[:count, span:],
+            result[count:, :span], result[count:, span:],
+        )
+
+    def spectrum(signals):
+        reals, imags = [], []
+        for signal in signals:
+            for ch in range(per):
+                high, low = split(signal[ch * parts : (ch + 1) * parts])
+                spec = dot(first_ref[...], jnp.concatenate([high, low, high], axis=0))
+                re, im = spec[:parts], spec[parts:]
+                reals.append(re * cosine + im * sine)
+                imags.append(im * cosine - re * sine)
+        rc, rs, ic, is_ = transform(jnp.concatenate(reals, axis=0), jnp.concatenate(imags, axis=0))
+        re, im = rc + is_, ic - rs
+        return [
+            (re[i * rows : (i + 1) * rows], im[i * rows : (i + 1) * rows])
+            for i in range(len(signals))
+        ]
+
     wait_blocks(filt_recv, parts - 1, sems.at[3])
-    stage[...] = recv[...].astype(jnp.float32).reshape(stage.shape)
     for s in range(parts):
         fstage[2 * per * s : 2 * per * (s + 1), :] = filt_recv[s]
+    ((fr, fi),) = spectrum([received(fstage, 2, 0)])
+
+    wait_blocks(recv, parts - 1, sems.at[1])
+    stage[...] = recv[...].astype(jnp.float32).reshape(stage.shape)
     signals = [received(stage, 8, a) for a in range(4)]
-    filt = received(fstage, 2, 0)
     grad = signals[3]
     moved = [[delayed(signals[b], j) for j in range(taps)] for b in range(3)]
     mixed = []
@@ -357,73 +390,31 @@
     query, key_part, value = mixed
     product = key_part * value
     dw = grad * query
-
-    cosine, sine = tw_ref[0], tw_ref[1]
-    reals, imags = [], []
-    for signal in (product, dw, filt):
-        for ch in range(per):
-            high, low = split(signal[ch * parts : (ch + 1) * parts])
-            spec = dot(first_ref[...], jnp.concatenate([high, low, high], axis=0))
-            re, im = spec[:parts], spec[parts:]
-            reals.append(re * cosine + im * sine)
-            imags.append(im * cosine - re * sine)
-
-    def transform(re, im):
-        both = jnp.concatenate([re, im], axis=0)
-        size = both.shape[0]
-        high, low = split(both)
-        result = dot(jnp.concatenate([high, low], axis=0), wide[0])
-        result = result[:size] + result[size:] + dot(high, wide[1])
-        count = size // 2
-        return (
-            result[:count, :span], result[:count, span:],
-            result[count:, :span], result[count:, span:],
+    (pr, pi), (dr, di) = spectrum([product, dw])
+
+    def inverse(spectra):
+        rc, rs, ic, is_ = transform(
+            jnp.concatenate([re for re, _ in spectra], axis=0),
+            jnp.concatenate([im for _, im in spectra], axis=0),
         )
-
-    rc, rs, ic, is_ = transform(jnp.concatenate(reals, axis=0), jnp.concatenate(imags, axis=0))
-    re, im = rc + is_, ic - rs
-    pr, dr, fr = (re[i * rows : (i + 1) * rows] for i in range(3))
-    pi, di, fi = (im[i * rows : (i + 1) * rows] for i in range(3))
-    out_r = jnp.concatenate([dr * pr + di * pi, fr * pr - fi * pi, dr * fr + di * fi], axis=0)
-    out_i = jnp.concatenate([di * pr - dr * pi, fr * pi + fi * pr, di * fr - dr * fi], axis=0)
-    rc, rs, ic, is_ = transform(out_r, out_i)
-    re, im = rc - is_, ic + rs
-
-    def finish(i):
-        blocks = []
-        for ch in range(per):
-            start = (i * per + ch) * parts
-            cr, ci = re[start : start + parts], im[start : start + parts]
-            both = jnp.concatenate([cr * cosine - ci * sine, ci * cosine + cr * sine], axis=0)
-            high, low = split(both)
-            blocks.append(dot(last_ref[...], jnp.concatenate([high, low, high], axis=0)))
-        return jnp.concatenate(blocks, axis=0)
-
-    corr = finish(0) * (total * groups) ** (-0.5)
-    for ch in range(per):
-        block = corr[ch * parts : (ch + 1) * parts]
-        fstage[pl.ds(2 * ch, parts, stride=2 * per), :] = block[:, :half]
-        fstage[pl.ds(2 * ch + 1, parts, stride=2 * per), :] = block[:, half:]
-    for s in range(parts):
-        fsend[s] = fstage[2 * per * s : 2 * per * (s + 1), :]
-    slot = group * share + me % share
-    for i in range(parts - 1, -1, -1):
-        peer = partner(me, i)
-        remote = push(fsend.at[peer], frecv.at[slot], 4, peer, target)
-        if i:
-            remote.start()
-        else:
-
-            @pl.when(target != group)
-            def _():
-                remote.start()
-
-            @pl.when(target == group)
-            def _():
-                pltpu.make_async_copy(fsend.at[me], frecv.at[slot], sems.at[5]).start()
-
-    conv_out = finish(1) + direct * product
-    dz = finish(2) + direct * dw
+        re, im = rc - is_, ic + rs
+        results = []
+        for i in range(len(spectra)):
+            blocks = []
+            for ch in range(per):
+                start = (i * per + ch) * parts
+                cr, ci = re[start : start + parts], im[start : start + parts]
+                both = jnp.concatenate([cr * cosine - ci * sine, ci * cosine + cr * sine], axis=0)
+                high, low = split(both)
+                blocks.append(dot(last_ref[...], jnp.concatenate([high, low, high], axis=0)))
+            results.append(jnp.concatenate(blocks, axis=0))
+        return results
+
+    conv_out, dz = inverse(
+        [(fr * pr - fi * pi, fr * pi + fi * pr), (dr * fr + di * fi, di * fr - dr * fi)]
+    )
+    conv_out = conv_out + direct * product
+    dz = dz + direct * dw
     grads = [grad * conv_out, dz * value, dz * key_part]
     for b in range(3):
         result = weight[b][0] * grads[b]
@@ -432,15 +423,27 @@
         for ch in range(per):
             block = result[ch * parts : (ch + 1) * parts]
             for h in (0, 1):
-                start = b * parts * 2 * per + 2 * ch + h
+                start = b * parts * 2 * per + h * per + ch
                 stage[pl.ds(start, parts, stride=2 * per), :] = block[:, h * half : (h + 1) * half]
         for s in range(parts):
-            start = (b * parts + s) * 2 * per
-            gsend[b, s] = stage[start : start + 2 * per, :]
-    pltpu.make_async_copy(gsend.at[:, me], grecv.at[:, me], sems.at[7]).start()
+            for h in (0, 1):
+                start = (b * parts + s) * 2 * per + h * per
+                gsend[s, b, h] = stage[start : start + per, :]
+    near = 8 // per
+    landing = grecv.at[:, me // near, :, me % near]
+    pltpu.make_async_copy(gsend.at[me], landing, sems.at[7]).start()
     for i in range(parts - 1, 0, -1):
         peer = partner(me, i)
-        push(gsend.at[:, peer], grecv.at[:, me], 6, peer, group).start()
+        push(gsend.at[peer], landing, 6, peer, group).start()
+
+    (corr,) = inverse([(dr * pr + di * pi, di * pr - dr * pi)])
+    corr = corr * (total * groups) ** (-0.5)
+    for ch in range(per):
+        block = corr[ch * parts : (ch + 1) * parts]
+        fstage[pl.ds(2 * ch, parts, stride=2 * per), :] = block[:, :half]
+        fstage[pl.ds(2 * ch + 1, parts, stride=2 * per), :] = block[:, half:]
+    for s in range(parts):
+        fsend[s] = fstage[2 * per * s : 2 * per * (s + 1), :]
 
     scale = total ** (-0.5)
     sums = [grads[b] * moved[b][j] for b in range(3) for j in range(taps)] + [dw * product]
@@ -453,6 +456,23 @@
             amount = jnp.sum(block, axis=1, keepdims=True) * scale
             line = jnp.where(spot == k * per + per * me + ch, amount, line)
     ssend[...] = line
+
+    slot = group * share + me % share
+    for i in range(parts - 1, -1, -1):
+        peer = partner(me, i)
+        remote = push(fsend.at[peer], frecv.at[slot], 4, peer, target)
+        if i:
+            remote.start()
+        else:
+
+            @pl.when(target != group)
+            def _():
+                remote.start()
+
+            @pl.when(target == group)
+            def _():
+                pltpu.make_async_copy(fsend.at[me], frecv.at[slot], sems.at[5]).start()
+
     pltpu.make_async_copy(ssend, srecv.at[me], sems.at[9]).start()
     for i in range(parts - 1, 0, -1):
         push(ssend, srecv.at[me], 8, partner(me, i), group).start()
@@ -468,37 +488,38 @@
     def _():
         wait_blocks(fsend, 1, sems.at[4])
 
-    part = gsend.at[:, pl.ds(0, parts - 1)]
-    pltpu.make_async_copy(part, part, sems.at[6]).wait()
+    wait_blocks(gsend, parts - 1, sems.at[6])
     wait_blocks(srecv, parts - 1, sems.at[8])
 
 
 def unpack_kernel(
-    groups, parts, grecv, frecv, srecv, ig_hbm, fg_hbm, skg_hbm, sg_hbm,
-    ig_ref, fg_ref, skg_ref, sg_ref, sems,
+    groups, parts, grecv, frecv_hbm, srecv_hbm, ig_hbm, fg_hbm, skg_hbm, sg_hbm,
+    frecv, srecv, fg_ref, skg_ref, sg_ref, sems,
 ):
     taps, channels = sg_ref.shape[1:]
-    half = grecv.shape[1]
+    half = grecv.shape[-1]
     per = channels // parts
     share = channels // groups
-
-    def save(n, src, dst):
-        copy = pltpu.make_async_copy(src, dst, sems.at[n])
-        copy.start()
-        return copy
-
+    copies = []
+
+    def copy(src, dst):
+        made = pltpu.make_async_copy(src, dst, sems.at[len(copies)])
+        made.start()
+        copies.append(made)
+        return made
+
+    loads = [copy(frecv_hbm, frecv), copy(srecv_hbm, srecv)]
     for b in range(3):
         for h in (0, 1):
-            ig_ref[b, :, h * half : (h + 1) * half] = grecv[
-                pl.ds(b * 2 * channels + h, channels, stride=2), :
-            ]
-    saves = [save(0, ig_ref, ig_hbm)]
+            copy(grecv.at[b, :, h], ig_hbm.at[b, :, :, pl.ds(h * half, half)])
+    loads[0].wait()
     for h in (0, 1):
         both = frecv[pl.ds(h, share, stride=2), :]
         for j in range(1, groups):
             both = both + frecv[pl.ds(2 * share * j + h, share, stride=2), :]
         fg_ref[:, h * half : (h + 1) * half] = both
-    saves.append(save(1, fg_ref, fg_hbm))
+    copy(fg_ref, fg_hbm)
+    loads[1].wait()
     sums = srecv[...]
     row = lax.broadcasted_iota(jnp.int32, sums.shape, 0)
     lane = lax.broadcasted_iota(jnp.int32, sums.shape, 1)
@@ -511,9 +532,10 @@
             sg_ref[k // taps, pl.ds(k % taps, 1), :] = piece
         else:
             skg_ref[...] = piece
-    saves += [save(2, skg_ref, skg_hbm), save(3, sg_ref, sg_hbm)]
-    for copy in saves:
-        copy.wait()
+    copy(skg_ref, skg_hbm)
+    copy(sg_ref, sg_hbm)
+    for made in copies[2:]:
+        made.wait()
 
 
 def owner_body(inputs, short_weights, filters, skip, grad_out):
@@ -532,7 +554,7 @@
     )
     limit = 60 * 1024 * 1024
     landing = (
-        jax.ShapeDtypeStruct((3, parts, 2 * per, half), f32),
+        jax.ShapeDtypeStruct((3, channels // 8, 2, 8 // per, per, half), f32),
         jax.ShapeDtypeStruct((parts, 2 * per, half), f32),
         jax.ShapeDtypeStruct((parts, 1, half), f32),
     )
@@ -556,7 +578,7 @@
             pltpu.VMEM((parts, 8 * per, half), jnp.bfloat16),
             pltpu.VMEM((parts, 2 * per, half), f32),
             pltpu.VMEM((parts, 2 * per, half), f32),
-            pltpu.VMEM((3, parts, 2 * per, half), f32),
+            pltpu.VMEM((parts, 3, 2, per, half), f32),
             pltpu.VMEM((parts, 2 * per, half), f32),
             pltpu.VMEM((1, half), f32),
             pltpu.VMEM((2 * channels, half), f32),
@@ -569,7 +591,7 @@
         name="owner_convolutions",
     )(*operands)
     shapes = (
-        jax.ShapeDtypeStruct((3, channels, span), f32),
+        jax.ShapeDtypeStruct((3, channels // 8, 8, span), f32),
         jax.ShapeDtypeStruct((channels // groups, span), f32),
         jax.ShapeDtypeStruct((1, channels), f32),
         jax.ShapeDtypeStruct((3, taps, channels), f32),
@@ -577,19 +599,22 @@
     in_grads, filter_grad, skip_grad, short_grad = pl.pallas_call(
         functools.partial(unpack_kernel, groups, parts),
         out_shape=shapes,
-        in_specs=[vmem] * 3,
+        in_specs=[hbm] * 3,
         out_specs=(hbm,) * 4,
         scratch_shapes=[
-            *[pltpu.VMEM(s.shape, f32) for s in shapes],
-            pltpu.SemaphoreType.DMA((4,)),
+            pltpu.VMEM((2 * channels, half), f32),
+            pltpu.VMEM((parts, half), f32),
+            *[pltpu.VMEM(s.shape, f32) for s in shapes[1:]],
+            pltpu.SemaphoreType.DMA((11,)),
         ],
         compiler_params=pltpu.CompilerParams(vmem_limit_bytes=limit),
         name="unpack_results",
     )(
-        blocks.reshape(6 * channels, half),
+        blocks.reshape(3, channels // 8, 2, 8, half),
         filter_blocks.reshape(2 * channels, half),
         sums.reshape(parts, half),
     )
+    in_grads = in_grads.reshape(3, channels, span)
     return in_grads, filter_grad, skip_grad.reshape(channels), short_grad
 
 

time: 20.9 us -> 23.7 us (1.13)
  Pallas kernels: 20.1 us -> 22.8 us
    pallas_call x1, Pallas kernels: 1.65 us -> 4.19 us  [owner_body(): pl.pallas_call(functools.partial(unpack_kernel, groups, parts), out_shape...]
where the time goes in v4:
time: 23.7 us; the launch traced here: 23.4 us
  Pallas kernels  22.8 us (96%)
  between operations  0.64 us (3%)
    pallas_call x1, Pallas kernels, owner_body(): pl.pallas_call(functools.partial(kernel, parts, groups), out_shape=landin...  18.6 us
    pallas_call x1, Pallas kernels, owner_body(): pl.pallas_call(functools.partial(unpack_kernel, groups, parts), out_shape...  4.19 us

profile of v4, /device:TPU:0, one launch (start us, length us, event | category | flops | bytes accessed | tf_op | source)
XLA Modules:
  0.0 23.4 jit_solution(16786666640895297215)
XLA Ops:
  0.6 18.6 %owner_convolutions.1 = (f32[3,4,2,4,2,128]{5,4,3,2,1,0:T(2,128)}, f32[16,4,128]{2,1,0:T(4,128)}, f32[16,1,128]{2,1,0:T(1,128)}) custom-call(bf16[3,32,256]{2,1,0:T(8,128)(2,1)} %x_hbm.1, bf16[32,256]{1,0:T(8,128)(2,1)} %g_hbm.1, f32[32,256]{1,0:T(8,128)} %f_hbm.1, f32[3,3,32]{2,1,0:T(4,128)} %sw_hbm.1, f32[32]{0:T(128)} %sk_hbm.1, ...), custom_call_target="tpu_custom_call" | custom-call | tf_op jit(solution)/shard_map/owner_convolutions/pallas_call | solution.py:561
  19.3 4.2 %unpack_results.1 = (f32[3,4,8,256]{3,2,1,0:T(8,128)}, f32[16,256]{1,0:T(8,128)}, f32[1,32]{1,0:T(1,128)}, f32[3,3,32]{2,1,0:T(4,128)}) custom-call(f32[3,4,2,8,128]{4,3,2,1,0:T(8,128)} %bitcast.5, f32[64,128]{1,0:T(8,128)} %bitcast.6, f32[16,128]{1,0:T(8,128)} %bitcast.7), custom_call_target="tpu_custom_call" | custom-call | tf_op jit(solution)/shard_map/unpack_results/pallas_call | solution.py:599

commit v5 on v4

--- a/solution.py
+++ b/solution.py
@@ -423,18 +423,15 @@
         for ch in range(per):
             block = result[ch * parts : (ch + 1) * parts]
             for h in (0, 1):
-                start = b * parts * 2 * per + h * per + ch
+                start = b * parts * 2 * per + 2 * ch + h
                 stage[pl.ds(start, parts, stride=2 * per), :] = block[:, h * half : (h + 1) * half]
         for s in range(parts):
-            for h in (0, 1):
-                start = (b * parts + s) * 2 * per + h * per
-                gsend[s, b, h] = stage[start : start + per, :]
-    near = 8 // per
-    landing = grecv.at[:, me // near, :, me % near]
-    pltpu.make_async_copy(gsend.at[me], landing, sems.at[7]).start()
+            start = (b * parts + s) * 2 * per
+            gsend[b, s] = stage[start : start + 2 * per, :]
+    pltpu.make_async_copy(gsend.at[:, me], grecv.at[:, me], sems.at[7]).start()
     for i in range(parts - 1, 0, -1):
         peer = partner(me, i)
-        push(gsend.at[peer], landing, 6, peer, group).start()
+        push(gsend.at[:, peer], grecv.at[:, me], 6, peer, group).start()
 
     (corr,) = inverse([(dr * pr + di * pi, di * pr - dr * pi)])
     corr = corr * (total * groups) ** (-0.5)
@@ -488,38 +485,37 @@
     def _():
         wait_blocks(fsend, 1, sems.at[4])
 
-    wait_blocks(gsend, parts - 1, sems.at[6])
+    part = gsend.at[:, pl.ds(0, parts - 1)]
+    pltpu.make_async_copy(part, part, sems.at[6]).wait()
     wait_blocks(srecv, parts - 1, sems.at[8])
 
 
 def unpack_kernel(
-    groups, parts, grecv, frecv_hbm, srecv_hbm, ig_hbm, fg_hbm, skg_hbm, sg_hbm,
-    frecv, srecv, fg_ref, skg_ref, sg_ref, sems,
+    groups, parts, grecv, frecv, srecv, ig_hbm, fg_hbm, skg_hbm, sg_hbm,
+    ig_ref, fg_ref, skg_ref, sg_ref, sems,
 ):
     taps, channels = sg_ref.shape[1:]
-    half = grecv.shape[-1]
+    half = grecv.shape[1]
     per = channels // parts
     share = channels // groups
-    copies = []
-
-    def copy(src, dst):
-        made = pltpu.make_async_copy(src, dst, sems.at[len(copies)])
-        made.start()
-        copies.append(made)
-        return made
-
-    loads = [copy(frecv_hbm, frecv), copy(srecv_hbm, srecv)]
+
+    def save(n, src, dst):
+        copy = pltpu.make_async_copy(src, dst, sems.at[n])
+        copy.start()
+        return copy
+
     for b in range(3):
         for h in (0, 1):
-            copy(grecv.at[b, :, h], ig_hbm.at[b, :, :, pl.ds(h * half, half)])
-    loads[0].wait()
+            ig_ref[b, :, h * half : (h + 1) * half] = grecv[
+                pl.ds(b * 2 * channels + h, channels, stride=2), :
+            ]
+    saves = [save(0, ig_ref, ig_hbm)]
     for h in (0, 1):
         both = frecv[pl.ds(h, share, stride=2), :]
         for j in range(1, groups):
             both = both + frecv[pl.ds(2 * share * j + h, share, stride=2), :]
         fg_ref[:, h * half : (h + 1) * half] = both
-    copy(fg_ref, fg_hbm)
-    loads[1].wait()
+    saves.append(save(1, fg_ref, fg_hbm))
     sums = srecv[...]
     row = lax.broadcasted_iota(jnp.int32, sums.shape, 0)
     lane = lax.broadcasted_iota(jnp.int32, sums.shape, 1)
@@ -532,10 +528,9 @@
             sg_ref[k // taps, pl.ds(k % taps, 1), :] = piece
         else:
             skg_ref[...] = piece
-    copy(skg_ref, skg_hbm)
-    copy(sg_ref, sg_hbm)
-    for made in copies[2:]:
-        made.wait()
+    saves += [save(2, skg_ref, skg_hbm), save(3, sg_ref, sg_hbm)]
+    for copy in saves:
+        copy.wait()
 
 
 def owner_body(inputs, short_weights, filters, skip, grad_out):
@@ -554,7 +549,7 @@
     )
     limit = 60 * 1024 * 1024
     landing = (
-        jax.ShapeDtypeStruct((3, channels // 8, 2, 8 // per, per, half), f32),
+        jax.ShapeDtypeStruct((3, parts, 2 * per, half), f32),
         jax.ShapeDtypeStruct((parts, 2 * per, half), f32),
         jax.ShapeDtypeStruct((parts, 1, half), f32),
     )
@@ -578,7 +573,7 @@
             pltpu.VMEM((parts, 8 * per, half), jnp.bfloat16),
             pltpu.VMEM((parts, 2 * per, half), f32),
             pltpu.VMEM((parts, 2 * per, half), f32),
-            pltpu.VMEM((parts, 3, 2, per, half), f32),
+            pltpu.VMEM((3, parts, 2 * per, half), f32),
             pltpu.VMEM((parts, 2 * per, half), f32),
             pltpu.VMEM((1, half), f32),
             pltpu.VMEM((2 * channels, half), f32),
@@ -591,7 +586,7 @@
         name="owner_convolutions",
     )(*operands)
     shapes = (
-        jax.ShapeDtypeStruct((3, channels // 8, 8, span), f32),
+        jax.ShapeDtypeStruct((3, channels, span), f32),
         jax.ShapeDtypeStruct((channels // groups, span), f32),
         jax.ShapeDtypeStruct((1, channels), f32),
         jax.ShapeDtypeStruct((3, taps, channels), f32),
@@ -599,22 +594,19 @@
     in_grads, filter_grad, skip_grad, short_grad = pl.pallas_call(
         functools.partial(unpack_kernel, groups, parts),
         out_shape=shapes,
-        in_specs=[hbm] * 3,
+        in_specs=[vmem] * 3,
         out_specs=(hbm,) * 4,
         scratch_shapes=[
-            pltpu.VMEM((2 * channels, half), f32),
-            pltpu.VMEM((parts, half), f32),
-            *[pltpu.VMEM(s.shape, f32) for s in shapes[1:]],
-            pltpu.SemaphoreType.DMA((11,)),
+            *[pltpu.VMEM(s.shape, f32) for s in shapes],
+            pltpu.SemaphoreType.DMA((4,)),
         ],
         compiler_params=pltpu.CompilerParams(vmem_limit_bytes=limit),
         name="unpack_results",
     )(
-        blocks.reshape(3, channels // 8, 2, 8, half),
+        blocks.reshape(6 * channels, half),
         filter_blocks.reshape(2 * channels, half),
         sums.reshape(parts, half),
     )
-    in_grads = in_grads.reshape(3, channels, span)
     return in_grads, filter_grad, skip_grad.reshape(channels), short_grad
 
 

time: 23.7 us -> 21.1 us (0.89)
  Pallas kernels: 22.8 us -> 20.3 us
    pallas_call x1, Pallas kernels: 4.19 us -> 1.65 us  [owner_body(): pl.pallas_call(functools.partial(unpack_kernel, groups, parts), out_shape...]
where the time goes in v5:
time: 21.1 us; the launch traced here: 20.9 us
  Pallas kernels  20.3 us (96%)
  between operations  0.64 us (3%)
    pallas_call x1, Pallas kernels, owner_body(): pl.pallas_call(functools.partial(kernel, parts, groups), out_shape=landin...  18.6 us
    pallas_call x1, Pallas kernels, owner_body(): pl.pallas_call(functools.partial(unpack_kernel, groups, parts), out_shape...  1.65 us

profile of v5, /device:TPU:0, one launch (start us, length us, event | category | flops | bytes accessed | tf_op | source)
XLA Modules:
  0.0 20.9 jit_solution(15499192084282381383)
XLA Ops:
  0.6 18.6 %owner_convolutions.1 = (f32[3,16,4,128]{3,2,1,0:T(4,128)}, f32[16,4,128]{2,1,0:T(4,128)}, f32[16,1,128]{2,1,0:T(1,128)}) custom-call(bf16[3,32,256]{2,1,0:T(8,128)(2,1)} %x_hbm.1, bf16[32,256]{1,0:T(8,128)(2,1)} %g_hbm.1, f32[32,256]{1,0:T(8,128)} %f_hbm.1, f32[3,3,32]{2,1,0:T(4,128)} %sw_hbm.1, f32[32]{0:T(128)} %sk_hbm.1, ...), custom_call_target="tpu_custom_call" | custom-call | tf_op jit(solution)/shard_map/owner_convolutions/pallas_call | solution.py:556
  19.2 1.6 %unpack_results.1 = (f32[3,32,256]{2,1,0:T(8,128)}, f32[16,256]{1,0:T(8,128)}, f32[1,32]{1,0:T(1,128)}, f32[3,3,32]{2,1,0:T(4,128)}) custom-call(f32[192,128]{1,0:T(8,128)} %bitcast.4, f32[64,128]{1,0:T(8,128)} %bitcast.5, f32[16,128]{1,0:T(8,128)} %bitcast.6), custom_call_target="tpu_custom_call" | custom-call | tf_op jit(solution)/shard_map/unpack_results/pallas_call | solution.py:594

commit v6 on v3

--- a/solution.py
+++ b/solution.py
@@ -216,9 +216,9 @@
 
 def kernel(
     parts, groups, x_hbm, g_hbm, f_hbm, sw_hbm, sk_hbm, wide_hbm, tw_hbm, first_hbm, last_hbm,
-    grecv, frecv, srecv,
+    grecv, frecv,
     x_ref, g_ref, f_ref, sw_ref, sk_ref, wide, tw_ref, first_ref, last_ref,
-    stage, send, recv, filt_send, filt_recv, gsend, fsend, ssend, fstage, sems, load_sems,
+    stage, send, recv, gsend, fsend, fstage, sems, load_sems,
 ):
     taps = sw_ref.shape[1]
     channels, span = f_ref.shape
@@ -261,13 +261,14 @@
         piece = piece.astype(jnp.float32)
         for h in (0, 1):
             stage[pl.ds(2 * a + h, channels, stride=8), :] = piece[:, h * half : (h + 1) * half]
-    send[...] = stage[...].astype(jnp.bfloat16).reshape(send.shape)
-    for h in (0, 1):
-        fstage[pl.ds(h, channels, stride=2), :] = f_ref[:, h * half : (h + 1) * half]
-    for s in range(parts):
-        filt_send[s] = fstage[2 * per * s : 2 * per * (s + 1), :]
+    for n, piece in enumerate(split(f_ref[...])):
+        piece = piece.astype(jnp.float32)
+        for h in (0, 1):
+            start = 2 * n + h
+            fstage[pl.ds(start, channels, stride=4), :] = piece[:, h * half : (h + 1) * half]
+    send[:, :per] = stage[...].reshape(parts, per, 8, half).astype(jnp.bfloat16)
+    send[:, per:] = fstage[...].reshape(parts, per // 2, 8, half).astype(jnp.bfloat16)
     recv[pl.ds(me, 1)] = send[pl.ds(me, 1)]
-    filt_recv[pl.ds(me, 1)] = filt_send[pl.ds(me, 1)]
 
     def push(src, dst, n, peer, chan):
         return pltpu.make_async_remote_copy(
@@ -286,7 +287,6 @@
     for i in range(parts - 1, 0, -1):
         peer = partner(me, i)
         push(send.at[peer], recv.at[me], 0, peer, group).start()
-        push(filt_send.at[peer], filt_recv.at[me], 2, peer, group).start()
 
     def wait_blocks(ref, count, sem):
         part = ref.at[pl.ds(0, count)]
@@ -340,12 +340,10 @@
     for load in loads[5:]:
         load.wait()
     wait_blocks(recv, parts - 1, sems.at[1])
-    wait_blocks(filt_recv, parts - 1, sems.at[3])
-    stage[...] = recv[...].astype(jnp.float32).reshape(stage.shape)
-    for s in range(parts):
-        fstage[2 * per * s : 2 * per * (s + 1), :] = filt_recv[s]
+    stage[...] = recv[:, :per].astype(jnp.float32).reshape(stage.shape)
+    fstage[...] = recv[:, per:].astype(jnp.float32).reshape(fstage.shape)
     signals = [received(stage, 8, a) for a in range(4)]
-    filt = received(fstage, 2, 0)
+    filt = received(fstage, 4, 0) + received(fstage, 4, 1)
     grad = signals[3]
     moved = [[delayed(signals[b], j) for j in range(taps)] for b in range(3)]
     mixed = []
@@ -432,15 +430,13 @@
         for ch in range(per):
             block = result[ch * parts : (ch + 1) * parts]
             for h in (0, 1):
-                start = b * parts * 2 * per + 2 * ch + h
-                stage[pl.ds(start, parts, stride=2 * per), :] = block[:, h * half : (h + 1) * half]
-        for s in range(parts):
-            start = (b * parts + s) * 2 * per
-            gsend[b, s] = stage[start : start + 2 * per, :]
-    pltpu.make_async_copy(gsend.at[:, me], grecv.at[:, me], sems.at[7]).start()
-    for i in range(parts - 1, 0, -1):
-        peer = partner(me, i)
-        push(gsend.at[:, peer], grecv.at[:, me], 6, peer, group).start()
+                start = (2 * b + h) * channels + ch
+                stage[pl.ds(start, parts, stride=per), :] = block[:, h * half : (h + 1) * half]
+            if ch == per - 1:
+                for n in (2 * b, 2 * b + 1):
+                    for s in range(parts):
+                        start = n * channels + s * per
+                        gsend[s, n] = stage[start : start + per, :]
 
     scale = total ** (-0.5)
     sums = [grads[b] * moved[b][j] for b in range(3) for j in range(taps)] + [dw * product]
@@ -452,30 +448,27 @@
             block = jnp.sum(folded[ch * parts : (ch + 1) * parts], axis=0, keepdims=True)
             amount = jnp.sum(block, axis=1, keepdims=True) * scale
             line = jnp.where(spot == k * per + per * me + ch, amount, line)
-    ssend[...] = line
-    pltpu.make_async_copy(ssend, srecv.at[me], sems.at[9]).start()
+    gsend[:, 6] = jnp.broadcast_to(line.reshape(1, 1, half), (parts, per, half))
+    pltpu.make_async_copy(gsend.at[me], grecv.at[me], sems.at[7]).start()
     for i in range(parts - 1, 0, -1):
-        push(ssend, srecv.at[me], 8, partner(me, i), group).start()
+        peer = partner(me, i)
+        push(gsend.at[peer], grecv.at[me], 6, peer, group).start()
 
     wait_blocks(frecv, parts, sems.at[5])
     pltpu.make_async_copy(grecv, grecv, sems.at[7]).wait()
-    wait_blocks(srecv, parts, sems.at[9])
     wait_blocks(send, parts - 1, sems.at[0])
-    wait_blocks(filt_send, parts - 1, sems.at[2])
     wait_blocks(fsend, parts - 1, sems.at[4])
 
     @pl.when(target != group)
     def _():
         wait_blocks(fsend, 1, sems.at[4])
 
-    part = gsend.at[:, pl.ds(0, parts - 1)]
-    pltpu.make_async_copy(part, part, sems.at[6]).wait()
-    wait_blocks(srecv, parts - 1, sems.at[8])
+    wait_blocks(gsend, parts - 1, sems.at[6])
 
 
 def unpack_kernel(
-    groups, parts, grecv, frecv, srecv, ig_hbm, fg_hbm, skg_hbm, sg_hbm,
-    ig_ref, fg_ref, skg_ref, sg_ref, sems,
+    groups, parts, grecv, frecv, ig_hbm, fg_hbm, skg_hbm, sg_hbm,
+    stage, ig_ref, fg_ref, skg_ref, sg_ref, sems,
 ):
     taps, channels = sg_ref.shape[1:]
     half = grecv.shape[1]
@@ -489,9 +482,12 @@
 
     for b in range(3):
         for h in (0, 1):
-            ig_ref[b, :, h * half : (h + 1) * half] = grecv[
-                pl.ds(b * 2 * channels + h, channels, stride=2), :
-            ]
+            n = 2 * b + h
+            for ch in range(per):
+                stage[pl.ds(n * channels + ch, parts, stride=per), :] = grecv[
+                    pl.ds(n * per + ch, parts, stride=7 * per), :
+                ]
+            ig_ref[b, :, h * half : (h + 1) * half] = stage[n * channels : (n + 1) * channels, :]
     saves = [save(0, ig_ref, ig_hbm)]
     for h in (0, 1):
         both = frecv[pl.ds(h, share, stride=2), :]
@@ -499,7 +495,7 @@
             both = both + frecv[pl.ds(2 * share * j + h, share, stride=2), :]
         fg_ref[:, h * half : (h + 1) * half] = both
     saves.append(save(1, fg_ref, fg_hbm))
-    sums = srecv[...]
+    sums = grecv[pl.ds(6 * per, parts, stride=7 * per), :]
     row = lax.broadcasted_iota(jnp.int32, sums.shape, 0)
     lane = lax.broadcasted_iota(jnp.int32, sums.shape, 1)
     for k in range(3 * taps + 1):
@@ -532,15 +528,14 @@
     )
     limit = 60 * 1024 * 1024
     landing = (
-        jax.ShapeDtypeStruct((3, parts, 2 * per, half), f32),
+        jax.ShapeDtypeStruct((parts, 7, per, half), f32),
         jax.ShapeDtypeStruct((parts, 2 * per, half), f32),
-        jax.ShapeDtypeStruct((parts, 1, half), f32),
-    )
-    blocks, filter_blocks, sums = pl.pallas_call(
+    )
+    blocks, filter_blocks = pl.pallas_call(
         functools.partial(kernel, parts, groups),
         out_shape=landing,
         in_specs=[hbm] * 9,
-        out_specs=(hbm,) * 3,
+        out_specs=(hbm,) * 2,
         scratch_shapes=[
             pltpu.VMEM(inputs.shape, inputs.dtype),
             pltpu.VMEM(grad_out.shape, grad_out.dtype),
@@ -552,14 +547,11 @@
             pltpu.VMEM(first.shape, first.dtype),
             pltpu.VMEM(last.shape, last.dtype),
             pltpu.VMEM((8 * channels, half), f32),
-            pltpu.VMEM((parts, 8 * per, half), jnp.bfloat16),
-            pltpu.VMEM((parts, 8 * per, half), jnp.bfloat16),
+            pltpu.VMEM((parts, per + per // 2, 8, half), jnp.bfloat16),
+            pltpu.VMEM((parts, per + per // 2, 8, half), jnp.bfloat16),
+            pltpu.VMEM((parts, 7, per, half), f32),
             pltpu.VMEM((parts, 2 * per, half), f32),
-            pltpu.VMEM((parts, 2 * per, half), f32),
-            pltpu.VMEM((3, parts, 2 * per, half), f32),
-            pltpu.VMEM((parts, 2 * per, half), f32),
-            pltpu.VMEM((1, half), f32),
-            pltpu.VMEM((2 * channels, half), f32),
+            pltpu.VMEM((4 * channels, half), f32),
             pltpu.SemaphoreType.DMA((10,)),
             pltpu.SemaphoreType.DMA((9,)),
         ],
@@ -577,18 +569,17 @@
     in_grads, filter_grad, skip_grad, short_grad = pl.pallas_call(
         functools.partial(unpack_kernel, groups, parts),
         out_shape=shapes,
-        in_specs=[vmem] * 3,
+        in_specs=[vmem] * 2,
         out_specs=(hbm,) * 4,
         scratch_shapes=[
+            pltpu.VMEM((6 * channels, half), f32),
             *[pltpu.VMEM(s.shape, f32) for s in shapes],
             pltpu.SemaphoreType.DMA((4,)),
         ],
         compiler_params=pltpu.CompilerParams(vmem_limit_bytes=limit),
         name="unpack_results",
     )(
-        blocks.reshape(6 * channels, half),
-        filter_blocks.reshape(2 * channels, half),
-        sums.reshape(parts, half),
+        blocks.reshape(7 * channels, half), filter_blocks.reshape(2 * channels, half)
     )
     return in_grads, filter_grad, skip_grad.reshape(channels), short_grad
 

time: 20.9 us -> 20.9 us (level)
  no operation moved by 1% of the time
where the time goes in v6:
time: 20.9 us; the launch traced here: 20.7 us
  Pallas kernels  20.1 us (96%)
  between operations  0.64 us (3%)
    pallas_call x1, Pallas kernels, owner_body(): pl.pallas_call(functools.partial(kernel, parts, groups), out_shape=landin...  18.4 us
    pallas_call x1, Pallas kernels, owner_body(): pl.pallas_call(functools.partial(unpack_kernel, groups, parts), out_shape...  1.63 us

profile of v6, /device:TPU:0, one launch (start us, length us, event | category | flops | bytes accessed | tf_op | source)
XLA Modules:
  0.0 20.7 jit_solution(15054621945574297859)
XLA Ops:
  0.6 18.4 %owner_convolutions.1 = (f32[16,7,2,128]{3,2,1,0:T(2,128)}, f32[16,4,128]{2,1,0:T(4,128)}) custom-call(bf16[3,32,256]{2,1,0:T(8,128)(2,1)} %x_hbm.1, bf16[32,256]{1,0:T(8,128)(2,1)} %g_hbm.1, f32[32,256]{1,0:T(8,128)} %f_hbm.1, f32[3,3,32]{2,1,0:T(4,128)} %sw_hbm.1, f32[32]{0:T(128)} %sk_hbm.1, bf16[2,256,512]{2,1,0:T(8,128)(2,1)} %constant.8.clone.wide_hbm, ...), custom_call_target="tpu_custom_call" | custom-call | tf_op jit(solution)/shard_map/owner_convolutions/pallas_call | solution.py:534
  19.1 1.6 %unpack_results.1 = (f32[3,32,256]{2,1,0:T(8,128)}, f32[16,256]{1,0:T(8,128)}, f32[1,32]{1,0:T(1,128)}, f32[3,3,32]{2,1,0:T(4,128)}) custom-call(f32[224,128]{1,0:T(8,128)} %bitcast.3, f32[64,128]{1,0:T(8,128)} %bitcast.4), custom_call_target="tpu_custom_call" | custom-call | tf_op jit(solution)/shard_map/unpack_results/pallas_call | solution.py:569

commit v7 on v6

--- a/solution.py
+++ b/solution.py
@@ -182,22 +182,23 @@
     return high, (table - high.astype(np.float32)).astype(jnp.bfloat16)
 
 
-def tables(parts, span):
+def tables(parts, span, count):
     period = 2 * parts * span
     u = np.arange(span)
     angle = 2.0 * np.pi / span * (u[:, None] * u[None, :] % span)
-    wide = np.concatenate([np.cos(angle), np.sin(angle)], axis=1)
-    wide = np.stack(split_table(wide))
+    high, low = split_table(np.concatenate([np.cos(angle), np.sin(angle)], axis=1))
+    wide = np.concatenate([high, high, low], axis=0)
     k = np.arange(parts) + 0.5
     angle = 2.0 * np.pi / period * k[:, None] * u[None, :]
-    twiddle = np.stack([np.cos(angle), np.sin(angle)]).astype(np.float32)
+    twiddle = np.stack([np.tile(np.cos(angle), (count, 1)), np.tile(np.sin(angle), (count, 1))])
     angle = np.pi / parts * k[:, None] * np.arange(parts)[None, :]
-    high, low = split_table(np.concatenate([np.cos(angle), -np.sin(angle)], axis=0))
+    each = np.eye(count)
+    cosine, sine = np.kron(each, np.cos(angle)), np.kron(each, np.sin(angle))
+    high, low = split_table(np.concatenate([cosine, -sine], axis=0))
     first = np.concatenate([high, high, low], axis=1)
-    last = np.concatenate([np.cos(angle).T, -np.sin(angle).T], axis=1) * (2.0 / period)
-    high, low = split_table(last)
+    high, low = split_table(np.concatenate([cosine.T, -sine.T], axis=1) * (2.0 / period))
     last = np.concatenate([high, high, low], axis=1)
-    return wide, twiddle, first, last
+    return wide, twiddle.astype(np.float32), first, last
 
 
 def partner(me, i):
@@ -357,28 +358,20 @@
     dw = grad * query
 
     cosine, sine = tw_ref[0], tw_ref[1]
-    reals, imags = [], []
-    for signal in (product, dw, filt):
-        for ch in range(per):
-            high, low = split(signal[ch * parts : (ch + 1) * parts])
-            spec = dot(first_ref[...], jnp.concatenate([high, low, high], axis=0))
-            re, im = spec[:parts], spec[parts:]
-            reals.append(re * cosine + im * sine)
-            imags.append(im * cosine - re * sine)
-
     def transform(re, im):
-        both = jnp.concatenate([re, im], axis=0)
-        size = both.shape[0]
-        high, low = split(both)
-        result = dot(jnp.concatenate([high, low], axis=0), wide[0])
-        result = result[:size] + result[size:] + dot(high, wide[1])
-        count = size // 2
+        high, low = split(jnp.concatenate([re, im], axis=0))
+        result = dot(jnp.concatenate([high, low, high], axis=1), wide[...])
+        count = result.shape[0] // 2
         return (
             result[:count, :span], result[:count, span:],
             result[count:, :span], result[count:, span:],
         )
 
-    rc, rs, ic, is_ = transform(jnp.concatenate(reals, axis=0), jnp.concatenate(imags, axis=0))
+    high, low = split(jnp.concatenate([product, dw, filt], axis=0))
+    spec = dot(first_ref[...], jnp.concatenate([high, low, high], axis=0))
+    count = spec.shape[0] // 2
+    re, im = spec[:count], spec[count:]
+    rc, rs, ic, is_ = transform(re * cosine + im * sine, im * cosine - re * sine)
     re, im = rc + is_, ic - rs
     pr, dr, fr = (re[i * rows : (i + 1) * rows] for i in range(3))
     pi, di, fi = (im[i * rows : (i + 1) * rows] for i in range(3))
@@ -386,18 +379,11 @@
     out_i = jnp.concatenate([di * pr - dr * pi, fr * pi + fi * pr, di * fr - dr * fi], axis=0)
     rc, rs, ic, is_ = transform(out_r, out_i)
     re, im = rc - is_, ic + rs
-
-    def finish(i):
-        blocks = []
-        for ch in range(per):
-            start = (i * per + ch) * parts
-            cr, ci = re[start : start + parts], im[start : start + parts]
-            both = jnp.concatenate([cr * cosine - ci * sine, ci * cosine + cr * sine], axis=0)
-            high, low = split(both)
-            blocks.append(dot(last_ref[...], jnp.concatenate([high, low, high], axis=0)))
-        return jnp.concatenate(blocks, axis=0)
-
-    corr = finish(0) * (total * groups) ** (-0.5)
+    both = jnp.concatenate([re * cosine - im * sine, im * cosine + re * sine], axis=0)
+    high, low = split(both)
+    fields = dot(last_ref[...], jnp.concatenate([high, low, high], axis=0))
+
+    corr = fields[:rows] * (total * groups) ** (-0.5)
     for ch in range(per):
         block = corr[ch * parts : (ch + 1) * parts]
         fstage[pl.ds(2 * ch, parts, stride=2 * per), :] = block[:, :half]
@@ -420,8 +406,8 @@
             def _():
                 pltpu.make_async_copy(fsend.at[me], frecv.at[slot], sems.at[5]).start()
 
-    conv_out = finish(1) + direct * product
-    dz = finish(2) + direct * dw
+    conv_out = fields[rows : 2 * rows] + direct * product
+    dz = fields[2 * rows :] + direct * dw
     grads = [grad * conv_out, dz * value, dz * key_part]
     for b in range(3):
         result = weight[b][0] * grads[b]
@@ -440,14 +426,16 @@
 
     scale = total ** (-0.5)
     sums = [grads[b] * moved[b][j] for b in range(3) for j in range(taps)] + [dw * product]
-    spot = lax.broadcasted_iota(jnp.int32, (1, half), 1)
-    line = jnp.zeros((1, half), jnp.float32)
+    spot = lax.broadcasted_iota(jnp.int32, (per * 16, half), 0)
+    table = jnp.zeros((per * 16, half), jnp.float32)
     for k, array in enumerate(sums):
         folded = array[:, :half] + array[:, half:]
         for ch in range(per):
             block = jnp.sum(folded[ch * parts : (ch + 1) * parts], axis=0, keepdims=True)
-            amount = jnp.sum(block, axis=1, keepdims=True) * scale
-            line = jnp.where(spot == k * per + per * me + ch, amount, line)
+            table = jnp.where(spot == k * per + ch, block, table)
+    table = jnp.sum(table, axis=1, keepdims=True) * scale
+    column = lax.broadcasted_iota(jnp.int32, (per * 16, half), 1)
+    line = jnp.sum(jnp.where(column == spot + per * me, table, 0.0), axis=0, keepdims=True)
     gsend[:, 6] = jnp.broadcast_to(line.reshape(1, 1, half), (parts, per, half))
     pltpu.make_async_copy(gsend.at[me], grecv.at[me], sems.at[7]).start()
     for i in range(parts - 1, 0, -1):
@@ -519,7 +507,7 @@
     channels, span = grad_out.shape
     per = channels // parts
     half = span // 2
-    wide, twiddle, first, last = (jnp.asarray(t) for t in tables(parts, span))
+    wide, twiddle, first, last = (jnp.asarray(t) for t in tables(parts, span, 3 * per))
     vmem = pl.BlockSpec(memory_space=pltpu.VMEM)
     hbm = pl.BlockSpec(memory_space=pltpu.HBM)
     f32 = jnp.float32

time: 20.9 us -> 20.9 us (level)
  no operation moved by 1% of the time
where the time goes in v7:
time: 20.9 us; the launch traced here: 20.7 us
  Pallas kernels  20.1 us (96%)
  between operations  0.64 us (3%)
    pallas_call x1, Pallas kernels, owner_body(): pl.pallas_call(functools.partial(kernel, parts, groups), out_shape=landin...  18.5 us
    pallas_call x1, Pallas kernels, owner_body(): pl.pallas_call(functools.partial(unpack_kernel, groups, parts), out_shape...  1.63 us

profile of v7, /device:TPU:0, one launch (start us, length us, event | category | flops | bytes accessed | tf_op | source)
XLA Modules:
  0.0 20.7 jit_solution(10242650789878015285)
XLA Ops:
  0.6 18.5 %owner_convolutions.1 = (f32[16,7,2,128]{3,2,1,0:T(2,128)}, f32[16,4,128]{2,1,0:T(4,128)}) custom-call(bf16[3,32,256]{2,1,0:T(8,128)(2,1)} %x_hbm.1, bf16[32,256]{1,0:T(8,128)(2,1)} %g_hbm.1, f32[32,256]{1,0:T(8,128)} %f_hbm.1, f32[3,3,32]{2,1,0:T(4,128)} %sw_hbm.1, f32[32]{0:T(128)} %sk_hbm.1, bf16[768,512]{1,0:T(8,128)(2,1)} %constant.8.clone.wide_hbm, ...), custom_call_target="tpu_custom_call" | custom-call | tf_op jit(solution)/shard_map/owner_convolutions/pallas_call | solution.py:522
  19.1 1.6 %unpack_results.1 = (f32[3,32,256]{2,1,0:T(8,128)}, f32[16,256]{1,0:T(8,128)}, f32[1,32]{1,0:T(1,128)}, f32[3,3,32]{2,1,0:T(4,128)}) custom-call(f32[224,128]{1,0:T(8,128)} %bitcast.3, f32[64,128]{1,0:T(8,128)} %bitcast.4), custom_call_target="tpu_custom_call" | custom-call | tf_op jit(solution)/shard_map/unpack_results/pallas_call | solution.py:557

commit v8 on v6

--- a/solution.py
+++ b/solution.py
@@ -200,14 +200,22 @@
     return wide, twiddle, first, last
 
 
-def partner(me, i):
+def partner(me, i, parts):
     peer = me
     bit = 1
-    while bit <= i:
-        if i & bit:
-            peer = peer + bit * (1 - 2 * (me // bit % 2))
+    while bit < parts:
+        step = bit * (1 - 2 * lax.rem(lax.div(me, bit), 2))
+        peer = peer + step * lax.rem(lax.div(i, bit), 2)
         bit *= 2
     return peer
+
+
+def each_partner(me, parts, act):
+    def step(n, carry):
+        act(partner(me, parts - 1 - n, parts))
+        return carry
+
+    lax.fori_loop(0, parts - 1, step, 0)
 
 
 def dot(a, b):
@@ -247,11 +255,14 @@
         )
 
     barrier = pltpu.get_barrier_semaphore()
-    for i in range(parts - 1, 0, -1):
-        greet(partner(me, i), group)
+    each_partner(me, parts, lambda peer: greet(peer, group))
     for j in range(1, groups):
-        for i in range(share):
-            greet(group * share + i, (group + j) % groups)
+
+        def greet_other(i, carry, j=j):
+            greet(group * share + i, lax.rem(group + j, groups))
+            return carry
+
+        lax.fori_loop(0, share, greet_other, 0)
     for load in loads[3:]:
         load.start()
     for load in loads[:3]:
@@ -284,9 +295,9 @@
     def _():
         pl.semaphore_wait(barrier, 2 * parts - 1)
 
-    for i in range(parts - 1, 0, -1):
-        peer = partner(me, i)
-        push(send.at[peer], recv.at[me], 0, peer, group).start()
+    each_partner(
+        me, parts, lambda peer: push(send.at[peer], recv.at[me], 0, peer, group).start()
+    )
 
     def wait_blocks(ref, count, sem):
         part = ref.at[pl.ds(0, count)]
@@ -405,20 +416,19 @@
     for s in range(parts):
         fsend[s] = fstage[2 * per * s : 2 * per * (s + 1), :]
     slot = group * share + me % share
-    for i in range(parts - 1, -1, -1):
-        peer = partner(me, i)
-        remote = push(fsend.at[peer], frecv.at[slot], 4, peer, target)
-        if i:
-            remote.start()
-        else:
-
-            @pl.when(target != group)
-            def _():
-                remote.start()
-
-            @pl.when(target == group)
-            def _():
-                pltpu.make_async_copy(fsend.at[me], frecv.at[slot], sems.at[5]).start()
+
+    def push_filter(peer):
+        return push(fsend.at[peer], frecv.at[slot], 4, peer, target)
+
+    each_partner(me, parts, lambda peer: push_filter(peer).start())
+
+    @pl.when(target != group)
+    def _():
+        push_filter(me).start()
+
+    @pl.when(target == group)
+    def _():
+        pltpu.make_async_copy(fsend.at[me], frecv.at[slot], sems.at[5]).start()
 
     conv_out = finish(1) + direct * product
     dz = finish(2) + direct * dw
@@ -450,9 +460,9 @@
             line = jnp.where(spot == k * per + per * me + ch, amount, line)
     gsend[:, 6] = jnp.broadcast_to(line.reshape(1, 1, half), (parts, per, half))
     pltpu.make_async_copy(gsend.at[me], grecv.at[me], sems.at[7]).start()
-    for i in range(parts - 1, 0, -1):
-        peer = partner(me, i)
-        push(gsend.at[peer], grecv.at[me], 6, peer, group).start()
+    each_partner(
+        me, parts, lambda peer: push(gsend.at[peer], grecv.at[me], 6, peer, group).start()
+    )
 
     wait_blocks(frecv, parts, sems.at[5])
     pltpu.make_async_copy(grecv, grecv, sems.at[7]).wait()

time: 20.9 us -> 21.7 us (1.038)
  Pallas kernels: 20.1 us -> 20.8 us
    pallas_call x1, Pallas kernels: 18.4 us -> 19.2 us  [owner_body(): pl.pallas_call(functools.partial(kernel, parts, groups), out_shape=landin...]
where the time goes in v8:
time: 21.7 us; the launch traced here: 21.5 us
  Pallas kernels  20.8 us (96%)
  between operations  0.64 us (3%)
    pallas_call x1, Pallas kernels, owner_body(): pl.pallas_call(functools.partial(kernel, parts, groups), out_shape=landin...  19.2 us
    pallas_call x1, Pallas kernels, owner_body(): pl.pallas_call(functools.partial(unpack_kernel, groups, parts), out_shape...  1.63 us

profile of v8, /device:TPU:0, one launch (start us, length us, event | category | flops | bytes accessed | tf_op | source)
XLA Modules:
  0.0 21.5 jit_solution(16634516983870518388)
XLA Ops:
  0.6 19.2 %owner_convolutions.1 = (f32[16,7,2,128]{3,2,1,0:T(2,128)}, f32[16,4,128]{2,1,0:T(4,128)}) custom-call(bf16[3,32,256]{2,1,0:T(8,128)(2,1)} %x_hbm.1, bf16[32,256]{1,0:T(8,128)(2,1)} %g_hbm.1, f32[32,256]{1,0:T(8,128)} %f_hbm.1, f32[3,3,32]{2,1,0:T(4,128)} %sw_hbm.1, f32[32]{0:T(128)} %sk_hbm.1, bf16[2,256,512]{2,1,0:T(8,128)(2,1)} %constant.8.clone.wide_hbm, ...), custom_call_target="tpu_custom_call" | custom-call | tf_op jit(solution)/shard_map/owner_convolutions/pallas_call | solution.py:544
  19.8 1.6 %unpack_results.1 = (f32[3,32,256]{2,1,0:T(8,128)}, f32[16,256]{1,0:T(8,128)}, f32[1,32]{1,0:T(1,128)}, f32[3,3,32]{2,1,0:T(4,128)}) custom-call(f32[224,128]{1,0:T(8,128)} %bitcast.3, f32[64,128]{1,0:T(8,128)} %bitcast.4), custom_call_target="tpu_custom_call" | custom-call | tf_op jit(solution)/shard_map/unpack_results/pallas_call | solution.py:579
